TPU v7x, 32 devices: a whole 2x2x4 slice. The times are simulated.
32 devices in a mesh: groups: 2 (over y), res: 4 (over z), blk: 2 (over x), ch: 2 (over core).
Axes of the slice: x: 2, y: 2, z: 4, core: 2. Of those that a mesh axis runs over, the one named last changes fastest.
Arguments:
- single: bfloat16 [16384, 384], P(('groups', 'res')), parts along dimension 0, may hold values from -6 to 6
- frames: float32 [12, 16384], P(None, ('groups', 'res')), parts along dimension 1
- teacher: float32 [12, 16384], P(None, ('groups', 'res')), parts along dimension 1
- res_mask: int32 [16384], P(('groups', 'res')), parts along dimension 0, may hold values 0 or 1
- chain_ids: int32 [16384], P(('groups', 'res')), parts along dimension 0, may hold values from 0 to 31, never falling along the last dimension, each value on 1 to 512 neighbouring positions
- block_pairs: int32 [16, 12, 2], P('groups'), parts along dimension 0, may hold values from 0 to 63, as said below
- w_left: bfloat16 [384, 128], replicated, may hold values from -0.3125 to 0.3125
- w_right: bfloat16 [384, 128], replicated, may hold values from -0.3125 to 0.3125
- w_value: bfloat16 [384, 128], replicated, may hold values from -0.3125 to 0.3125
- w_pair: bfloat16 [128, 128], P(None, 'ch'), may hold values from -0.5 to 0.5
- pair_bias: float32 [128], P('ch'), may hold values from -3 to 3
- gate_vec: float32 [128], P('ch'), may hold values from -1 to 1
- w_out: bfloat16 [128, 384], replicated, may hold values from -0.5 to 0.5
Outputs:
- updated: bfloat16 [16384, 384], P(('groups', 'res')), parts along dimension 0
- pair_fape: float32 [192], P(('groups', 'res', 'blk')), parts along dimension 0
There are 2 independent parts, one for each index of `groups`. A program takes and returns all parts, laid end to end along the dimension named above; an argument that names none is the same for every part. Nothing has to cross between parts.
Inputs may be any that keep to these rules, and one draw needn't show every extreme that they name: block_pairs[o,p,0] lies in blocks (o // 2) * 16 to (o // 2 + 1) * 16 - 1. Among the 12 pairs of one owner at most 4 have their second block in one run of blocks k * 16 to (k+1) * 16 - 1, and in every draw each owner has exactly 4 in one such run.
All inputs are finite; a program needn't handle non-finite values. No bound on the sum of `res_mask` on one device may be relied on, other than what follows from the above.
Results may differ from a plain program's by a relative error of at most 0.0059.
Values may be sent and summed in bfloat16 or wider, within the bound.
A program may use at most 64 MiB of HBM per device.

v0:
```python
import jax
import jax.numpy as jnp
from jax import lax
from jax.sharding import PartitionSpec as P

BLOCK = 128


def tile_logit(near_left, far_right, w_pair, pair_bias, gate_vec):
    outer_prod = (
        near_left.astype(jnp.float32)[:, :, None] * far_right.astype(jnp.float32).T[None, :, :]
    ).astype(jnp.bfloat16)
    pair_act = jnp.einsum("kc,akb->acb", w_pair, outer_prod, preferred_element_type=jnp.float32)
    pair_act = pair_act + pair_bias[None, :, None]
    return jnp.einsum(
        "c,acb->ab", gate_vec, jnp.maximum(pair_act, 0.0), precision=lax.Precision.HIGHEST
    )


def local_coords(geo_near, geo_far, offset):
    coords = []
    for axis_k in range(3):
        summed = jnp.zeros(
            geo_near.shape[:-2] + (geo_near.shape[-1], geo_far.shape[-1]), jnp.float32
        )
        for axis_m in range(3):
            gap_vec = (
                geo_far[..., offset + 9 + axis_m, None, :]
                - geo_near[..., offset + 9 + axis_m, :, None]
            )
            summed = summed + geo_near[..., offset + 3 * axis_m + axis_k, :, None] * gap_vec
        coords.append(summed)
    return coords


def finish(logit, value_near, value_far, geo_near, geo_far):
    live = geo_near[..., 24, :, None] * geo_far[..., 24, None, :]
    live = live * (geo_near[..., 25, :, None] != geo_far[..., 25, None, :]).astype(jnp.float32)
    weight = jax.nn.sigmoid(logit) * live
    weight_low = weight.astype(jnp.bfloat16)
    scale = BLOCK ** (-0.5)
    to_second = jnp.einsum(
        "pab,pac->pbc", weight_low, value_near, preferred_element_type=jnp.float32
    )
    to_second = (to_second * scale).astype(jnp.bfloat16)
    to_first = jnp.einsum("pab,pbc->pac", weight_low, value_far, preferred_element_type=jnp.float32)
    to_first = (to_first * scale).astype(jnp.bfloat16)
    pred_coords = local_coords(geo_near, geo_far, 0)
    true_coords = local_coords(geo_near, geo_far, 12)
    dist_sq = jnp.zeros_like(weight)
    for axis_k in range(3):
        dist_sq = dist_sq + (pred_coords[axis_k] - true_coords[axis_k]) ** 2
    clipped = jnp.minimum(jnp.sqrt(dist_sq + 0.0001), 10.0)
    fape_value = jnp.sum(weight * clipped, axis=(1, 2)) / (BLOCK * BLOCK)
    return (fape_value, to_first, to_second)


def shards(
    single,
    frames,
    teacher,
    res_mask,
    chain_ids,
    block_pairs,
    w_left,
    w_right,
    w_value,
    w_pair,
    pair_bias,
    gate_vec,
    w_out,
):
    res_count = lax.axis_size("res")
    blk_count = lax.axis_size("blk")
    res_rank = lax.axis_index("res")
    blk_rank = lax.axis_index("blk")
    row_count = single.shape[0]
    feat_width = single.shape[1]
    blocks_here = row_count // BLOCK
    pair_dev = block_pairs.shape[1]
    capacity = 1 + (pair_dev + res_count - 2) // res_count
    msg_width = w_value.shape[1]
    owner_table = block_pairs.reshape(res_count, blk_count, pair_dev, 2)
    column_pairs = lax.dynamic_index_in_dim(owner_table, blk_rank, 1, keepdims=False)
    own_pairs = lax.dynamic_index_in_dim(column_pairs, res_rank, 0, keepdims=False)
    wanted_ids = column_pairs[:, :, 1]
    hit_flags = (wanted_ids // blocks_here == res_rank).astype(jnp.int32)
    hit_rank = jnp.cumsum(hit_flags, axis=1) - 1
    slot_ids = jnp.arange(capacity, dtype=jnp.int32)
    picked = hit_flags[:, None, :] * (hit_rank[:, None, :] == slot_ids[None, :, None]).astype(
        jnp.int32
    )
    send_local = jnp.sum(
        picked * (wanted_ids - res_rank * blocks_here)[:, None, :], axis=2
    ).reshape(-1)
    send_valid = jnp.sum(picked, axis=2).reshape(-1)
    geometry = jnp.concatenate(
        [
            frames,
            teacher,
            res_mask[None, :].astype(jnp.float32),
            chain_ids[None, :].astype(jnp.float32),
        ],
        axis=0,
    )
    geo_blocks = geometry.reshape(26, blocks_here, BLOCK).transpose(1, 0, 2)
    geo_send = jnp.take(geo_blocks, send_local, axis=0).reshape(res_count, capacity, 26, BLOCK)
    first_local = own_pairs[:, 0] - res_rank * blocks_here
    source_shard = own_pairs[:, 1] // blocks_here
    pair_index = jnp.arange(pair_dev, dtype=jnp.int32)
    earlier = (source_shard[None, :] == source_shard[:, None]) & (
        pair_index[None, :] < pair_index[:, None]
    )
    recv_slot = source_shard * capacity + jnp.sum(earlier.astype(jnp.int32), axis=1)
    single_blocks = single.reshape(blocks_here, BLOCK, feat_width)
    row_send = jnp.take(single_blocks, send_local, axis=0).reshape(
        res_count, capacity, BLOCK, feat_width
    )
    row_recv = lax.all_to_all(row_send, "res", split_axis=0, concat_axis=0, tiled=True)
    far_rows = jnp.take(row_recv.reshape(-1, BLOCK, feat_width), recv_slot, axis=0)
    near_rows = jnp.take(single_blocks, first_local, axis=0)
    left_feats = jnp.einsum(
        "pad,dc->pac", near_rows, w_left, preferred_element_type=jnp.float32
    ).astype(jnp.bfloat16)
    value_near = jnp.einsum(
        "pad,dc->pac", near_rows, w_value, preferred_element_type=jnp.float32
    ).astype(jnp.bfloat16)
    right_feats = jnp.einsum(
        "pad,dc->pac", far_rows, w_right, preferred_element_type=jnp.float32
    ).astype(jnp.bfloat16)
    value_far = jnp.einsum(
        "pad,dc->pac", far_rows, w_value, preferred_element_type=jnp.float32
    ).astype(jnp.bfloat16)
    geo_recv = lax.all_to_all(
        geo_send.astype(jnp.bfloat16), "res", split_axis=0, concat_axis=0, tiled=True
    ).astype(geo_send.dtype)
    far_geo = jnp.take(geo_recv.reshape(-1, 26, BLOCK), recv_slot, axis=0)
    near_geo = jnp.take(geo_blocks, first_local, axis=0)

    def tile_step(state_in, tile_inputs):
        return (state_in, tile_logit(tile_inputs[0], tile_inputs[1], w_pair, pair_bias, gate_vec))

    state_out, partial_logits = lax.scan(
        tile_step, jnp.zeros((), jnp.float32), (left_feats, right_feats)
    )
    logits = lax.psum(partial_logits, "ch")
    pair_fape, to_first, to_second = finish(logits, value_near, value_far, near_geo, far_geo)
    back_hot = (
        recv_slot[:, None] == jnp.arange(res_count * capacity, dtype=jnp.int32)[None, :]
    ).astype(jnp.bfloat16)
    back_buffer = jnp.einsum(
        "ps,pbc->sbc", back_hot, to_second, preferred_element_type=jnp.float32
    ).astype(jnp.bfloat16)
    back_buffer = back_buffer.reshape(res_count, capacity, BLOCK, msg_width)
    returned = lax.all_to_all(back_buffer, "res", split_axis=0, concat_axis=0, tiled=True)
    block_index = jnp.arange(blocks_here, dtype=jnp.int32)
    send_hot = ((send_local[:, None] == block_index[None, :]) & (send_valid[:, None] > 0)).astype(
        jnp.bfloat16
    )
    delta_rows = jnp.einsum(
        "sl,sbc->lbc",
        send_hot,
        returned.reshape(-1, BLOCK, msg_width),
        preferred_element_type=jnp.float32,
    )
    near_hot = (first_local[:, None] == block_index[None, :]).astype(jnp.bfloat16)
    delta_rows = delta_rows + jnp.einsum(
        "pl,pac->lac", near_hot, to_first, preferred_element_type=jnp.float32
    )
    delta_rows = delta_rows.reshape(row_count, msg_width)
    summed_rows = lax.psum(delta_rows, "blk")
    updated = (
        single.astype(jnp.float32)
        + jnp.dot(summed_rows.astype(jnp.bfloat16), w_out, preferred_element_type=jnp.float32)
    ).astype(jnp.bfloat16)
    return (updated, pair_fape)


def solution(mesh):
    placed = (
        P(("groups", "res"), None),
        P(None, ("groups", "res")),
        P(None, ("groups", "res")),
        P(("groups", "res")),
        P(("groups", "res")),
        P("groups", None, None),
        P(),
        P(),
        P(),
        P(None, "ch"),
        P("ch"),
        P("ch"),
        P(),
    )
    return jax.shard_map(
        shards,
        mesh=mesh,
        in_specs=placed,
        out_specs=(P(("groups", "res"), None), P(("groups", "res", "blk"))),
        check_vma=False,
    )
```

profile of v0, /device:TPU:0, one launch (start us, length us, event | category | flops | bytes accessed | tf_op | source)
XLA Modules:
  0.0 224.0 jit_solution(8328334812829523707)
XLA Ops:
  8.9 2.3 %gather_fusion = bf16[16,128,384]{2,1,0:T(8,128)(2,1)S(1)} fusion(bf16[16,128,384]{2,1,0:T(8,128)(2,1)} %bitcast.219, s32[1024]{0:T(1024)S(1)} %pad_clamp_fusion.1), kind=kCustom, calls=%fused_computation.4 | custom fusion | bytes 3145792 | tf_op jit(solution)/shard_map/jit(_take)/gather | solution.py:116
  11.3 1.4 broadcast_select_fusion
  12.7 6.4 %all-to-all-start = ((bf16[4,4,128,384]{3,2,1,0:T(8,128)(2,1)}), bf16[4,4,128,384]{3,2,1,0:T(8,128)(2,1)S(1)}, u32[]{:S(2)}, u32[]{:S(2)}) async-start(bf16[4,4,128,384]{3,2,1,0:T(8,128)(2,1)} %broadcast_select_fusion), calls=%async_computation | async-start | bytes 3145728 | tf_op jit(solution)/shard_map/all_to_all | solution.py:119
  20.5 1.8 gather_fusion.2
  22.6 1.2 gather_fusion.1
  23.8 1.2 gather_fusion.4
  25.8 1.0 broadcast_select_fusion.10
  28.1 1.7 fusion.42
  29.8 2.6 %convolution_convert_fusion.4 = bf16[12,128,128]{2,1,0:T(8,128)(2,1)} fusion(bf16[12,128,384]{2,1,0:T(8,128)(2,1)} %gather_fusion.2, pred[12]{0:T(512)(128)(4,1)} %copy-done.26, bf16[384,128]{1,0:T(8,128)(2,1)} %param.25), kind=kOutput, calls=%fused_computation.52 | convolution fusion | flops 151781376 | bytes 1671180 | tf_op jit(solution)/shard_map/pad,dc->pac/dot_general | solution.py:122
  32.3 23.7 %all-to-all-done = bf16[4,4,128,384]{3,2,1,0:T(8,128)(2,1)S(1)} async-done(((bf16[4,4,128,384]{3,2,1,0:T(8,128)(2,1)}), bf16[4,4,128,384]{3,2,1,0:T(8,128)(2,1)S(1)}, u32[]{:S(2)}, u32[]{:S(2)}) %all-to-all-start) | async-done | bytes 1572896 | tf_op jit(solution)/shard_map/all_to_all | solution.py:119
  56.1 3.3 %all-to-all-start.1 = ((bf16[4,4,26,128]{3,1,2,0:T(4,128)(2,1)}), bf16[4,4,26,128]{3,1,2,0:T(4,128)(2,1)S(1)}, u32[]{:S(2)}, u32[]{:S(2)}) async-start(bf16[4,4,26,128]{3,1,2,0:T(4,128)(2,1)} %fusion.42), calls=%async_computation.1 | async-start | bytes 212992 | tf_op jit(solution)/shard_map/all_to_all | solution.py:134
  59.4 1.8 gather_fusion.3
  61.2 1.8 convolution_convert_fusion.3
  63.1 79.4 %while.11 = (s32[]{:T(128)}, f32[12,128,128]{2,1,0:T(8,128)}, bf16[12,128,128]{2,1,0:T(8,128)(2,1)}, bf16[12,128,128]{2,1,0:T(8,128)(2,1)S(1)}, bf16[128,64]{0,1...) while((s32[]{:T(128)}, f32[12,128,128]{2,1,0:T(8,128)}, bf16[12,128,128]{2,1,0:T(8,128)(2,1)}, ...), condition=%wide.region_5.7_spmd.clone, body=%wide.region_4.6_spmd.sunk.clone | while | flops 287342592 | bytes 9061461 | solution.py:143
  64.1 2.5 %fusion.98 = f32[128,128,64]{1,2,0:T(8,128)S(1)} fusion(f32[128,128]{1,0:T(8,128)S(1)} %convert_bitcast_fusion.3, f32[128,128]{1,0:T(8,128)S(1)} %bitcast_convert_fusion.3, bf16[128,64]{0,1:T(8,128)(2,1)S(1)} %get-tuple-element.198), kind=kOutput, calls=%fused_computation.7.clone.1.clone | convolution fusion | flops 272629760 | bytes 4341760 | tf_op jit(solution)/shard_map/while/body/eval_jaxpr/kc,akb->acb/dot_general | solution.py:13
  66.6 2.5 %fusion.99 = f32[1,128,128]{2,0,1:T(1,128)S(1)} fusion(f32[128,128,64]{1,2,0:T(8,128)S(1)} %fusion.98, f32[64]{0:T(128)S(1)} %get-tuple-element.199, f32[64]{0:T(128)S(1)} %get-tuple-element.200), kind=kOutput, calls=%fused_computation.8.clone.1.clone | convolution fusion | flops 14680064 | bytes 4260352 | tf_op jit(solution)/shard_map/while/body/eval_jaxpr/c,acb->ab/dot_general | solution.py:15
  69.9 0.8 bitcast_convert_fusion.3
  70.7 2.5 %fusion.98 = f32[128,128,64]{1,2,0:T(8,128)S(1)} fusion(f32[128,128]{1,0:T(8,128)S(1)} %convert_bitcast_fusion.3, f32[128,128]{1,0:T(8,128)S(1)} %bitcast_convert_fusion.3, bf16[128,64]{0,1:T(8,128)(2,1)S(1)} %get-tuple-element.198), kind=kOutput, calls=%fused_computation.7.clone.1.clone | convolution fusion | flops 272629760 | bytes 4341760 | tf_op jit(solution)/shard_map/while/body/eval_jaxpr/kc,akb->acb/dot_general | solution.py:13
  73.2 2.5 %fusion.99 = f32[1,128,128]{2,0,1:T(1,128)S(1)} fusion(f32[128,128,64]{1,2,0:T(8,128)S(1)} %fusion.98, f32[64]{0:T(128)S(1)} %get-tuple-element.199, f32[64]{0:T(128)S(1)} %get-tuple-element.200), kind=kOutput, calls=%fused_computation.8.clone.1.clone | convolution fusion | flops 14680064 | bytes 4260352 | tf_op jit(solution)/shard_map/while/body/eval_jaxpr/c,acb->ab/dot_general | solution.py:15
  77.3 2.5 %fusion.98 = f32[128,128,64]{1,2,0:T(8,128)S(1)} fusion(f32[128,128]{1,0:T(8,128)S(1)} %convert_bitcast_fusion.3, f32[128,128]{1,0:T(8,128)S(1)} %bitcast_convert_fusion.3, bf16[128,64]{0,1:T(8,128)(2,1)S(1)} %get-tuple-element.198), kind=kOutput, calls=%fused_computation.7.clone.1.clone | convolution fusion | flops 272629760 | bytes 4341760 | tf_op jit(solution)/shard_map/while/body/eval_jaxpr/kc,akb->acb/dot_general | solution.py:13
  79.8 2.5 %fusion.99 = f32[1,128,128]{2,0,1:T(1,128)S(1)} fusion(f32[128,128,64]{1,2,0:T(8,128)S(1)} %fusion.98, f32[64]{0:T(128)S(1)} %get-tuple-element.199, f32[64]{0:T(128)S(1)} %get-tuple-element.200), kind=kOutput, calls=%fused_computation.8.clone.1.clone | convolution fusion | flops 14680064 | bytes 4260352 | tf_op jit(solution)/shard_map/while/body/eval_jaxpr/c,acb->ab/dot_general | solution.py:15
  83.9 2.5 %fusion.98 = f32[128,128,64]{1,2,0:T(8,128)S(1)} fusion(f32[128,128]{1,0:T(8,128)S(1)} %convert_bitcast_fusion.3, f32[128,128]{1,0:T(8,128)S(1)} %bitcast_convert_fusion.3, bf16[128,64]{0,1:T(8,128)(2,1)S(1)} %get-tuple-element.198), kind=kOutput, calls=%fused_computation.7.clone.1.clone | convolution fusion | flops 272629760 | bytes 4341760 | tf_op jit(solution)/shard_map/while/body/eval_jaxpr/kc,akb->acb/dot_general | solution.py:13
  86.5 2.5 %fusion.99 = f32[1,128,128]{2,0,1:T(1,128)S(1)} fusion(f32[128,128,64]{1,2,0:T(8,128)S(1)} %fusion.98, f32[64]{0:T(128)S(1)} %get-tuple-element.199, f32[64]{0:T(128)S(1)} %get-tuple-element.200), kind=kOutput, calls=%fused_computation.8.clone.1.clone | convolution fusion | flops 14680064 | bytes 4260352 | tf_op jit(solution)/shard_map/while/body/eval_jaxpr/c,acb->ab/dot_general | solution.py:15
  90.5 2.5 %fusion.98 = f32[128,128,64]{1,2,0:T(8,128)S(1)} fusion(f32[128,128]{1,0:T(8,128)S(1)} %convert_bitcast_fusion.3, f32[128,128]{1,0:T(8,128)S(1)} %bitcast_convert_fusion.3, bf16[128,64]{0,1:T(8,128)(2,1)S(1)} %get-tuple-element.198), kind=kOutput, calls=%fused_computation.7.clone.1.clone | convolution fusion | flops 272629760 | bytes 4341760 | tf_op jit(solution)/shard_map/while/body/eval_jaxpr/kc,akb->acb/dot_general | solution.py:13
  93.1 2.5 %fusion.99 = f32[1,128,128]{2,0,1:T(1,128)S(1)} fusion(f32[128,128,64]{1,2,0:T(8,128)S(1)} %fusion.98, f32[64]{0:T(128)S(1)} %get-tuple-element.199, f32[64]{0:T(128)S(1)} %get-tuple-element.200), kind=kOutput, calls=%fused_computation.8.clone.1.clone | convolution fusion | flops 14680064 | bytes 4260352 | tf_op jit(solution)/shard_map/while/body/eval_jaxpr/c,acb->ab/dot_general | solution.py:15
  97.2 2.5 %fusion.98 = f32[128,128,64]{1,2,0:T(8,128)S(1)} fusion(f32[128,128]{1,0:T(8,128)S(1)} %convert_bitcast_fusion.3, f32[128,128]{1,0:T(8,128)S(1)} %bitcast_convert_fusion.3, bf16[128,64]{0,1:T(8,128)(2,1)S(1)} %get-tuple-element.198), kind=kOutput, calls=%fused_computation.7.clone.1.clone | convolution fusion | flops 272629760 | bytes 4341760 | tf_op jit(solution)/shard_map/while/body/eval_jaxpr/kc,akb->acb/dot_general | solution.py:13
  99.7 2.5 %fusion.99 = f32[1,128,128]{2,0,1:T(1,128)S(1)} fusion(f32[128,128,64]{1,2,0:T(8,128)S(1)} %fusion.98, f32[64]{0:T(128)S(1)} %get-tuple-element.199, f32[64]{0:T(128)S(1)} %get-tuple-element.200), kind=kOutput, calls=%fused_computation.8.clone.1.clone | convolution fusion | flops 14680064 | bytes 4260352 | tf_op jit(solution)/shard_map/while/body/eval_jaxpr/c,acb->ab/dot_general | solution.py:15
  103.8 2.5 %fusion.98 = f32[128,128,64]{1,2,0:T(8,128)S(1)} fusion(f32[128,128]{1,0:T(8,128)S(1)} %convert_bitcast_fusion.3, f32[128,128]{1,0:T(8,128)S(1)} %bitcast_convert_fusion.3, bf16[128,64]{0,1:T(8,128)(2,1)S(1)} %get-tuple-element.198), kind=kOutput, calls=%fused_computation.7.clone.1.clone | convolution fusion | flops 272629760 | bytes 4341760 | tf_op jit(solution)/shard_map/while/body/eval_jaxpr/kc,akb->acb/dot_general | solution.py:13
  106.3 2.5 %fusion.99 = f32[1,128,128]{2,0,1:T(1,128)S(1)} fusion(f32[128,128,64]{1,2,0:T(8,128)S(1)} %fusion.98, f32[64]{0:T(128)S(1)} %get-tuple-element.199, f32[64]{0:T(128)S(1)} %get-tuple-element.200), kind=kOutput, calls=%fused_computation.8.clone.1.clone | convolution fusion | flops 14680064 | bytes 4260352 | tf_op jit(solution)/shard_map/while/body/eval_jaxpr/c,acb->ab/dot_general | solution.py:15
  110.4 2.5 %fusion.98 = f32[128,128,64]{1,2,0:T(8,128)S(1)} fusion(f32[128,128]{1,0:T(8,128)S(1)} %convert_bitcast_fusion.3, f32[128,128]{1,0:T(8,128)S(1)} %bitcast_convert_fusion.3, bf16[128,64]{0,1:T(8,128)(2,1)S(1)} %get-tuple-element.198), kind=kOutput, calls=%fused_computation.7.clone.1.clone | convolution fusion | flops 272629760 | bytes 4341760 | tf_op jit(solution)/shard_map/while/body/eval_jaxpr/kc,akb->acb/dot_general | solution.py:13
  112.9 2.5 %fusion.99 = f32[1,128,128]{2,0,1:T(1,128)S(1)} fusion(f32[128,128,64]{1,2,0:T(8,128)S(1)} %fusion.98, f32[64]{0:T(128)S(1)} %get-tuple-element.199, f32[64]{0:T(128)S(1)} %get-tuple-element.200), kind=kOutput, calls=%fused_computation.8.clone.1.clone | convolution fusion | flops 14680064 | bytes 4260352 | tf_op jit(solution)/shard_map/while/body/eval_jaxpr/c,acb->ab/dot_general | solution.py:15
  117.0 2.5 %fusion.98 = f32[128,128,64]{1,2,0:T(8,128)S(1)} fusion(f32[128,128]{1,0:T(8,128)S(1)} %convert_bitcast_fusion.3, f32[128,128]{1,0:T(8,128)S(1)} %bitcast_convert_fusion.3, bf16[128,64]{0,1:T(8,128)(2,1)S(1)} %get-tuple-element.198), kind=kOutput, calls=%fused_computation.7.clone.1.clone | convolution fusion | flops 272629760 | bytes 4341760 | tf_op jit(solution)/shard_map/while/body/eval_jaxpr/kc,akb->acb/dot_general | solution.py:13
  119.5 2.5 %fusion.99 = f32[1,128,128]{2,0,1:T(1,128)S(1)} fusion(f32[128,128,64]{1,2,0:T(8,128)S(1)} %fusion.98, f32[64]{0:T(128)S(1)} %get-tuple-element.199, f32[64]{0:T(128)S(1)} %get-tuple-element.200), kind=kOutput, calls=%fused_computation.8.clone.1.clone | convolution fusion | flops 14680064 | bytes 4260352 | tf_op jit(solution)/shard_map/while/body/eval_jaxpr/c,acb->ab/dot_general | solution.py:15
  123.6 2.5 %fusion.98 = f32[128,128,64]{1,2,0:T(8,128)S(1)} fusion(f32[128,128]{1,0:T(8,128)S(1)} %convert_bitcast_fusion.3, f32[128,128]{1,0:T(8,128)S(1)} %bitcast_convert_fusion.3, bf16[128,64]{0,1:T(8,128)(2,1)S(1)} %get-tuple-element.198), kind=kOutput, calls=%fused_computation.7.clone.1.clone | convolution fusion | flops 272629760 | bytes 4341760 | tf_op jit(solution)/shard_map/while/body/eval_jaxpr/kc,akb->acb/dot_general | solution.py:13
  126.2 2.5 %fusion.99 = f32[1,128,128]{2,0,1:T(1,128)S(1)} fusion(f32[128,128,64]{1,2,0:T(8,128)S(1)} %fusion.98, f32[64]{0:T(128)S(1)} %get-tuple-element.199, f32[64]{0:T(128)S(1)} %get-tuple-element.200), kind=kOutput, calls=%fused_computation.8.clone.1.clone | convolution fusion | flops 14680064 | bytes 4260352 | tf_op jit(solution)/shard_map/while/body/eval_jaxpr/c,acb->ab/dot_general | solution.py:15
  130.3 2.5 %fusion.98 = f32[128,128,64]{1,2,0:T(8,128)S(1)} fusion(f32[128,128]{1,0:T(8,128)S(1)} %convert_bitcast_fusion.3, f32[128,128]{1,0:T(8,128)S(1)} %bitcast_convert_fusion.3, bf16[128,64]{0,1:T(8,128)(2,1)S(1)} %get-tuple-element.198), kind=kOutput, calls=%fused_computation.7.clone.1.clone | convolution fusion | flops 272629760 | bytes 4341760 | tf_op jit(solution)/shard_map/while/body/eval_jaxpr/kc,akb->acb/dot_general | solution.py:13
  132.8 2.5 %fusion.99 = f32[1,128,128]{2,0,1:T(1,128)S(1)} fusion(f32[128,128,64]{1,2,0:T(8,128)S(1)} %fusion.98, f32[64]{0:T(128)S(1)} %get-tuple-element.199, f32[64]{0:T(128)S(1)} %get-tuple-element.200), kind=kOutput, calls=%fused_computation.8.clone.1.clone | convolution fusion | flops 14680064 | bytes 4260352 | tf_op jit(solution)/shard_map/while/body/eval_jaxpr/c,acb->ab/dot_general | solution.py:15
  136.9 2.5 %fusion.98 = f32[128,128,64]{1,2,0:T(8,128)S(1)} fusion(f32[128,128]{1,0:T(8,128)S(1)} %convert_bitcast_fusion.3, f32[128,128]{1,0:T(8,128)S(1)} %bitcast_convert_fusion.3, bf16[128,64]{0,1:T(8,128)(2,1)S(1)} %get-tuple-element.198), kind=kOutput, calls=%fused_computation.7.clone.1.clone | convolution fusion | flops 272629760 | bytes 4341760 | tf_op jit(solution)/shard_map/while/body/eval_jaxpr/kc,akb->acb/dot_general | solution.py:13
  139.4 2.5 %fusion.99 = f32[1,128,128]{2,0,1:T(1,128)S(1)} fusion(f32[128,128,64]{1,2,0:T(8,128)S(1)} %fusion.98, f32[64]{0:T(128)S(1)} %get-tuple-element.199, f32[64]{0:T(128)S(1)} %get-tuple-element.200), kind=kOutput, calls=%fused_computation.8.clone.1.clone | convolution fusion | flops 14680064 | bytes 4260352 | tf_op jit(solution)/shard_map/while/body/eval_jaxpr/c,acb->ab/dot_general | solution.py:15
  151.7 11.7 %all-reduce.3.cloned.1.call-done = f32[12,128,128]{2,1,0:T(8,128)} async-done(((f32[12,128,128]{2,1,0:T(8,128)}), f32[12,128,128]{2,1,0:T(8,128)}) %all-reduce.3.cloned.1.call-update) | async-done | bytes 786448 | tf_op jit(solution)/shard_map/psum | solution.py:146
  163.4 2.0 fusion.12
  165.8 1.0 copy.48
  166.8 4.9 %all-to-all-start.2 = ((bf16[4,4,128,128]{3,1,2,0:T(4,128)(2,1)}), bf16[4,4,128,128]{3,1,2,0:T(4,128)(2,1)S(1)}, u32[]{:S(2)}, u32[]{:S(2)}) async-start(bf16[4,4,128,128]{3,1,2,0:T(4,128)(2,1)} %copy.48), calls=%async_computation.2 | async-start | bytes 1048576 | tf_op jit(solution)/shard_map/all_to_all | solution.py:155
  171.7 7.5 %fusion.38 = f32[12]{0:T(128)S(1)} fusion(f32[12,128]{1,0:T(8,128)S(1)} %bitcast.233, f32[12,128]{1,0:T(8,128)S(1)} %bitcast.234, f32[12,128]{1,0:T(8,128)S(1)} %bitcast.235, f32[12,128]{1,0:T(8,128)S(1)} %bitcast.236, f32[12,128]{1,0:T(8,128)S(1)} %bitcast.240, f32[12,128]{1,0:T(8,128)S(1)} %bitcast.244, f32[12,128]{1,0:T(8,128)S(1)} %bitcast.245, ...), kind=kLoop, calls=%fused_computation.80 | loop fusion | flops 10813428 | bytes 995376 | tf_op jit(solution)/shard_map/reduce_sum | solution.py:54
  179.7 2.7 %fusion.13 = bf16[12,128,128]{2,1,0:T(8,128)(2,1)} fusion(bf16[12,128,384]{2,1,0:T(8,128)(2,1)S(1)} %copy-done.3, pred[12]{0:T(512)(128)(4,1)} %copy-done.25, bf16[384,128]{1,0:T(8,128)(2,1)} %param.27, f32[12,128,128]{2,1,0:T(8,128)} %all-reduce.3.cloned.1.call-done, f32[12,128]{1,0:T(8,128)} %bitcast.265, f32[12,128]{1,0:T(8,128)S(1)} %bitcast.239, ...), kind=kOutput, calls=%fused_computation.48 | convolution fusion | flops 204079104 | bytes 2482188 | tf_op jit(solution)/shard_map/pab,pbc->pac/dot_general | solution.py:46
  182.4 4.2 %all-to-all-done.2 = bf16[4,4,128,128]{3,1,2,0:T(4,128)(2,1)S(1)} async-done(((bf16[4,4,128,128]{3,1,2,0:T(4,128)(2,1)}), bf16[4,4,128,128]{3,1,2,0:T(4,128)(2,1)S(1)}, u32[]{:S(2)}, u32[]{:S(2)}) %all-to-all-start.2) | async-done | bytes 524320 | tf_op jit(solution)/shard_map/all_to_all | solution.py:155
  187.8 27.6 %all-reduce.4 = bf16[2048,128]{1,0:T(8,128)(2,1)S(1)} all-reduce(f32[2048,128]{1,0:T(8,128)S(1)} %bitcast.224), channel_id=1, replica_groups=mesh['groups'=2,'res'=4,'blk'=2,'ch'=2] {'blk'}, use_global_device_ids=true, to_apply=%region_7.10 | all-reduce | flops 262144 | bytes 1572864 | tf_op jit(solution)/shard_map/psum | solution.py:171
  215.5 1.7 add_convert_fusion
  (200 shorter events, 33.8 us)
Async XLA Ops:
  7.2 208.3 %copy-start = (bf16[128,384]{1,0:T(8,128)(2,1)S(1)}, bf16[128,384]{1,0:T(8,128)(2,1)}, u32[]{:S(2)}) copy-start(bf16[128,384]{1,0:T(8,128)(2,1)} %param.31) | copy-start | bytes 294916
  8.9 2.3 %copy-start.19 = (pred[4,4]{1,0:T(4,128)(4,1)}, pred[4,4]{1,0:T(4,128)(4,1)S(1)}, u32[]{:S(2)}) copy-start(pred[4,4]{1,0:T(4,128)(4,1)S(1)} %compare_and_fusion.2) | copy-start | bytes 52
  12.7 7.8 %copy-start.1 = (bf16[2048,384]{1,0:T(8,128)(2,1)S(1)}, bf16[2048,384]{1,0:T(8,128)(2,1)}, u32[]{:S(2)}) copy-start(bf16[2048,384]{1,0:T(8,128)(2,1)} %param.19) | copy-start | bytes 4718596
  12.7 43.4 %all-to-all-start = ((bf16[4,4,128,384]{3,2,1,0:T(8,128)(2,1)}), bf16[4,4,128,384]{3,2,1,0:T(8,128)(2,1)S(1)}, u32[]{:S(2)}, u32[]{:S(2)}) async-start(bf16[4,4,128,384]{3,2,1,0:T(8,128)(2,1)} %broadcast_select_fusion), calls=%async_computation | async-start | bytes 3145728 | tf_op jit(solution)/shard_map/all_to_all | solution.py:119
  19.1 3.2 %copy-start.6 = (f32[12,2048]{1,0:T(8,128)S(1)}, f32[12,2048]{1,0:T(8,128)}, u32[]{:S(2)}) copy-start(f32[12,2048]{1,0:T(8,128)} %param.20) | copy-start | bytes 294916
  19.1 3.3 %copy-start.7 = (f32[12,2048]{1,0:T(8,128)S(1)}, f32[12,2048]{1,0:T(8,128)}, u32[]{:S(2)}) copy-start(f32[12,2048]{1,0:T(8,128)} %param.21) | copy-start | bytes 294916
  19.8 5.2 %copy-start.22 = (s32[12,2]{0,1:T(2,128)}, s32[12,2]{0,1:T(2,128)S(1)}, u32[]{:S(2)}) copy-start(s32[12,2]{0,1:T(2,128)S(1)} %dynamic-slice_bitcast_fusion) | copy-start | bytes 292
  19.8 0.6 copy-start.20
  19.9 5.9 %copy-start.26 = (pred[12]{0:T(512)(128)(4,1)}, pred[12]{0:T(512)(128)(4,1)S(1)}, u32[]{:S(2)}) copy-start(pred[12]{0:T(512)(128)(4,1)S(1)} %get-tuple-element.81) | copy-start | bytes 40
  20.4 2.0 copy-start.16
  20.5 2.0 copy-start.17
  25.2 0.6 copy-start.28
  25.8 35.4 %copy-start.25 = (pred[12]{0:T(512)(128)(4,1)}, pred[12]{0:T(512)(128)(4,1)S(1)}, u32[]{:S(2)}) copy-start(pred[12]{0:T(512)(128)(4,1)S(1)} %get-tuple-element.79) | copy-start | bytes 40
  25.8 33.6 %copy-start.18 = (s32[1024]{0:T(1024)}, s32[1024]{0:T(1024)S(1)}, u32[]{:S(2)}) copy-start(s32[1024]{0:T(1024)S(1)} %pad_clamp_fusion) | copy-start | bytes 12292
  56.1 90.5 %all-to-all-start.1 = ((bf16[4,4,26,128]{3,1,2,0:T(4,128)(2,1)}), bf16[4,4,26,128]{3,1,2,0:T(4,128)(2,1)S(1)}, u32[]{:S(2)}, u32[]{:S(2)}) async-start(bf16[4,4,26,128]{3,1,2,0:T(4,128)(2,1)} %fusion.42), calls=%async_computation.1 | async-start | bytes 212992 | tf_op jit(solution)/shard_map/all_to_all | solution.py:134
  59.4 104.0 %all-reduce.3.cloned.1.call-start = ((), (), s32[]{:S(2)}) async-start(), calls=%async_computation.3 | async-start | bytes 1572864 | tf_op jit(solution)/shard_map/psum | solution.py:146
  61.2 1.9 copy-start.5
  61.2 1.9 copy-start.13
  61.2 1.9 copy-start.14
  63.1 79.5 %copy-start.15 = (s32[4,4]{1,0:T(4,128)S(1)}, s32[4,4]{1,0:T(4,128)}, u32[]{:S(2)}) copy-start(s32[4,4]{1,0:T(4,128)} %get-tuple-element.63) | copy-start | bytes 196
  63.1 80.2 %copy-start.12 = (f32[12,1,128]{2,1,0:T(1,128)S(1)}, f32[12,1,128]{2,1,0:T(1,128)}, u32[]{:S(2)}) copy-start(f32[12,1,128]{2,1,0:T(1,128)} %get-tuple-element.97) | copy-start | bytes 18436
  63.1 80.3 %copy-start.11 = (f32[12,1,128]{2,1,0:T(1,128)S(1)}, f32[12,1,128]{2,1,0:T(1,128)}, u32[]{:S(2)}) copy-start(f32[12,1,128]{2,1,0:T(1,128)} %get-tuple-element.111) | copy-start | bytes 18436
  63.1 80.3 %copy-start.10 = (f32[12,1,128]{2,1,0:T(1,128)S(1)}, f32[12,1,128]{2,1,0:T(1,128)}, u32[]{:S(2)}) copy-start(f32[12,1,128]{2,1,0:T(1,128)} %get-tuple-element.112) | copy-start | bytes 18436
  63.1 83.4 %copy-start.23 = (s32[12,2]{0,1:T(2,128)S(1)}, s32[12,2]{0,1:T(2,128)}, u32[]{:S(2)}) copy-start(s32[12,2]{0,1:T(2,128)} %copy-done.22) | copy-start | bytes 292
  63.1 83.4 %copy-start.29 = (s32[12]{0:T(128)S(1)}, s32[12]{0:T(128)}, u32[]{:S(2)}) copy-start(s32[12]{0:T(128)} %copy-done.28) | copy-start | bytes 148
  142.6 20.8 %copy-start.2 = (bf16[12,128,384]{2,1,0:T(8,128)(2,1)S(1)}, bf16[12,128,384]{2,1,0:T(8,128)(2,1)}, u32[]{:S(2)}) copy-start(bf16[12,128,384]{2,1,0:T(8,128)(2,1)} %gather_fusion.2) | copy-start | bytes 3538948
  151.6 13.8 %copy-start.8 = (f32[12,1,128]{2,0,1:T(8,128)}, f32[12,1,128]{2,0,1:T(8,128)S(1)}, u32[]{:S(2)}) copy-start(f32[12,1,128]{2,0,1:T(8,128)S(1)} %copy.163) | copy-start | bytes 18436
  151.7 13.8 %copy-start.9 = (f32[12,1,128]{2,0,1:T(8,128)}, f32[12,1,128]{2,0,1:T(8,128)S(1)}, u32[]{:S(2)}) copy-start(f32[12,1,128]{2,0,1:T(8,128)S(1)} %copy.165) | copy-start | bytes 18436
  165.8 13.9 %copy-start.3 = (bf16[12,128,384]{2,1,0:T(8,128)(2,1)S(1)}, bf16[12,128,384]{2,1,0:T(8,128)(2,1)}, u32[]{:S(2)}) copy-start(bf16[12,128,384]{2,1,0:T(8,128)(2,1)} %gather_fusion.3) | copy-start | bytes 3538948
  166.8 19.8 %all-to-all-start.2 = ((bf16[4,4,128,128]{3,1,2,0:T(4,128)(2,1)}), bf16[4,4,128,128]{3,1,2,0:T(4,128)(2,1)S(1)}, u32[]{:S(2)}, u32[]{:S(2)}) async-start(bf16[4,4,128,128]{3,1,2,0:T(4,128)(2,1)} %copy.48), calls=%async_computation.2 | async-start | bytes 1048576 | tf_op jit(solution)/shard_map/all_to_all | solution.py:155
  179.7 7.1 %copy-start.24 = (s32[16]{0:T(128)S(1)}, s32[16]{0:T(128)}, u32[]{:S(2)}) copy-start(s32[16]{0:T(128)} %eq.90) | copy-start | bytes 196
  179.7 7.1 %copy-start.27 = (pred[16]{0:T(512)(128)(4,1)S(1)}, pred[16]{0:T(512)(128)(4,1)}, u32[]{:S(2)}) copy-start(pred[16]{0:T(512)(128)(4,1)} %gt.12) | copy-start | bytes 52
  182.4 4.7 %copy-start.4 = (bf16[12,128,128]{2,1,0:T(8,128)(2,1)S(1)}, bf16[12,128,128]{2,1,0:T(8,128)(2,1)}, u32[]{:S(2)}) copy-start(bf16[12,128,128]{2,1,0:T(8,128)(2,1)} %fusion.13) | copy-start | bytes 1179652
  182.4 4.7 %copy-start.21 = (s32[12]{0:T(128)S(1)}, s32[12]{0:T(128)}, u32[]{:S(2)}) copy-start(s32[12]{0:T(128)} %copy-done.20) | copy-start | bytes 148
Sparse Core Ops, SparseCore 0:
  142.7 20.5 all-reduce.2
where the time goes:
time: 225 us; the launch traced here: 224 us
  matrix products  72.7 us (32%)
  waiting for transfers between devices  39.6 us (18%)
  local copies, waits for them, and re-layouts  31 us (14%)
  blocking collectives  27.6 us (12%)
  other arithmetic  23.4 us (10%)
  starting transfers between devices  14.7 us (7%)
  between operations  14.7 us (7%)
    dot_general x12, matrix products, tile_logit(): jnp.einsum('c,acb->ab', gate_vec, jnp.maximum(pair_act, 0.0), precision=l...  30.6 us
    dot_general x12, matrix products, tile_logit(): jnp.einsum('kc,akb->acb', w_pair, outer_prod, preferred_element_type=jnp....  30.3 us
    psum x1, blocking collectives, shards(): summed_rows = lax.psum(delta_rows, 'blk')  27.6 us
    all_to_all x1, waiting for transfers between devices, shards(): lax.all_to_all(row_send, 'res', split_axis=0, concat_axis=0, tiled=True)  23.7 us
    psum x1, waiting for transfers between devices, shards(): logits = lax.psum(partial_logits, 'ch')  11.7 us
    convert_element_type x12, other arithmetic, tile_logit(): near_left.astype(jnp.float32)[:, :, None]  9.25 us
    dynamic_update_slice x12, local copies, waits for them, and re-layouts, shards(): lax.scan(tile_step, jnp.zeros((), jnp.float32), (left_feats, right_feats))  7.54 us
    reduce_sum x1, other arithmetic, finish(): fape_value = jnp.sum(weight * clipped, axis=(1, 2)) / (BLOCK * BLOCK)  7.52 us
  transfers between devices with their start and end apart: 4, of which 3 were waited for; matrix products, arithmetic and copies ran while one was open for 51% of the time, Pallas kernels for 0%

commit v1 on v0

v1 whole, which is shorter than its diff:
```python
import functools
import jax
import jax.numpy as jnp
from jax import lax
from jax.experimental import pallas as pl
from jax.experimental.pallas import tpu as pltpu
from jax.sharding import PartitionSpec as P

BLOCK = 128
CHUNK = 8
MESH = pl.DeviceIdType.MESH


def pair_kernel(
    sizes,
    pairs_ref,
    single_ref,
    frames_ref,
    teacher_ref,
    mask_ref,
    chain_ref,
    w_left_ref,
    w_right_ref,
    w_value_ref,
    gate_in_ref,
    w_out_ref,
    updated_ref,
    fape_ref,
    left_ref,
    value_ref,
    right_ref,
    geo_ref,
    far_geo_ref,
    pack_ref,
    w_bcast_ref,
    floor_ref,
    gate_ref,
    send_tab,
    near_tab,
    valid_tab,
    pos_tab,
    send_ref,
    recv_ref,
    geo_send_ref,
    geo_recv_ref,
    rhs_ref,
    logit_ref,
    geo_t_ref,
    weight_ref,
    first_ref,
    back_send_ref,
    back_recv_ref,
    delta_ref,
    half_send_ref,
    half_recv_ref,
    cross_send_ref,
    cross_recv_ref,
    low_own_ref,
    low_other_ref,
    fape_own_ref,
    fape_other_ref,
    w_sems,
    row_send_sem,
    row_recv_sem,
    geo_send_sem,
    geo_recv_sem,
    back_send_sem,
    back_recv_sem,
    half_sems,
    cross_send_sem,
    cross_recv_sem,
    low_send_sem,
    low_recv_sem,
    fape_sems,
):
    res_count, blk_count, blocks, pair_dev, slots, chans, parts = sizes
    total = res_count * slots
    half = blocks // 2
    piece = half // parts
    res = lax.axis_index("res")
    blk = lax.axis_index("blk")
    core = lax.axis_index("ch")
    f32, bf16 = jnp.float32, jnp.bfloat16

    barrier = pltpu.get_barrier_semaphore()

    def greet(step, carry):
        pl.semaphore_signal(
            barrier,
            inc=1,
            device_id={"res": lax.rem(res + step, res_count)},
            device_id_type=MESH,
        )
        return carry

    lax.fori_loop(1, res_count, greet, 0)
    pl.semaphore_signal(barrier, inc=1, device_id={"ch": 1 - core}, device_id_type=MESH)
    for step in range(1, blk_count):
        pl.semaphore_signal(
            barrier,
            inc=1,
            device_id={"blk": lax.rem(blk + step, blk_count)},
            device_id_type=MESH,
        )

    pack_ref[0] = gate_in_ref[...]

    def lookup(owner, shard):
        base = owner * (pair_dev * 2)
        zero = jnp.int32(0)
        rank = zero
        found = [[zero, zero, zero, zero] for _ in range(slots)]
        for p in range(pair_dev):
            first = pairs_ref[base + 2 * p]
            second = pairs_ref[base + 2 * p + 1]
            hit = (second >= shard * blocks) & (second < (shard + 1) * blocks)
            for j in range(slots):
                match = hit & (rank == 2 * j + core)
                old = found[j]
                found[j] = [
                    jnp.where(match, jnp.clip(first - res * blocks, 0, blocks - 1), old[0]),
                    jnp.where(match, second - shard * blocks, old[1]),
                    jnp.where(match, 1, old[2]),
                    jnp.where(match, p, old[3]),
                ]
            rank = rank + jnp.where(hit, 1, 0)
        return found

    def fill_tables(d, carry):
        out = lookup(lax.rem(res + d, res_count) * blk_count + blk, res)
        own = lookup(res * blk_count + blk, lax.rem(res - d + res_count, res_count))
        for j in range(slots):
            send_tab[d * slots + j] = out[j][1]
            near_tab[d * slots + j] = own[j][0]
            valid_tab[d * slots + j] = own[j][2]
            pos_tab[d * slots + j] = own[j][3]
        return carry

    lax.fori_loop(0, res_count, fill_tables, 0)

    def features(n, carry):
        rows = single_ref[pl.ds(pl.multiple_of(n * BLOCK, BLOCK), BLOCK), :]
        left_ref[n] = jnp.dot(rows, w_left_ref[...], preferred_element_type=f32).astype(bf16)
        right_ref[n] = jnp.dot(rows, w_right_ref[...], preferred_element_type=f32).astype(bf16)
        value_ref[n] = jnp.dot(rows, w_value_ref[...], preferred_element_type=f32).astype(bf16)
        lanes = pl.ds(pl.multiple_of(n * BLOCK, BLOCK), BLOCK)
        frames = frames_ref[:, lanes]
        teacher = teacher_ref[:, lanes]
        mask = mask_ref[:, lanes].astype(f32)
        chain = chain_ref[:, lanes].astype(f32)
        geo_ref[n] = jnp.concatenate(
            [frames, teacher, mask, chain, jnp.zeros((6, BLOCK), f32)], axis=0
        )
        far_geo_ref[n] = jnp.concatenate([frames[9:12], teacher[9:12], mask, chain], axis=0)
        return carry

    lax.fori_loop(0, blocks, features, 0)

    pl.semaphore_wait(barrier, res_count + blk_count - 1)

    w_copy = pltpu.make_async_remote_copy(
        src_ref=pack_ref.at[0],
        dst_ref=pack_ref.at[1],
        send_sem=w_sems.at[0],
        recv_sem=w_sems.at[1],
        device_id={"ch": 1 - core},
        device_id_type=MESH,
    )
    w_copy.start()

    def row_copies(d):
        target = {"res": lax.rem(res + d, res_count)}
        return (
            pltpu.make_async_remote_copy(
                src_ref=send_ref.at[d],
                dst_ref=recv_ref.at[d],
                send_sem=row_send_sem.at[d],
                recv_sem=row_recv_sem.at[d],
                device_id=target,
                device_id_type=MESH,
            ),
            pltpu.make_async_remote_copy(
                src_ref=geo_send_ref.at[d],
                dst_ref=geo_recv_ref.at[d],
                send_sem=geo_send_sem.at[d],
                recv_sem=geo_recv_sem.at[d],
                device_id=target,
                device_id_type=MESH,
            ),
        )

    def assemble(d, rows_to, geo_to):
        for j in range(slots):
            n = send_tab[d * slots + j]
            rows_to[d, j, :, 0:BLOCK] = right_ref[n]
            rows_to[d, j, :, BLOCK : 2 * BLOCK] = value_ref[n]
            geo_to[d, j] = far_geo_ref[n]

    def send_rows(d, carry):
        assemble(d, send_ref, geo_send_ref)
        for copy in row_copies(d):
            copy.start()
        return carry

    lax.fori_loop(1, res_count, send_rows, 0)
    assemble(0, recv_ref, geo_recv_ref)

    w_copy.wait()
    for h in range(2):
        floor_ref[h * chans : (h + 1) * chans, :] = jnp.concatenate(
            [pack_ref[h, 1]] * 2, axis=1
        )
        gate_ref[h * chans : (h + 1) * chans, :] = jnp.concatenate(
            [pack_ref[h, 2]] * 2, axis=1
        )
        for c in range(chans):
            row = jnp.broadcast_to(pack_ref[h, 0, c : c + 1, :], (16, BLOCK)).astype(bf16)
            w_bcast_ref[h * chans + c] = jnp.concatenate([row, row], axis=1)
    offset = -jnp.sum(floor_ref[:, 0:BLOCK] * gate_ref[:, 0:BLOCK], axis=0, keepdims=True)
    rhs_ref[...] = jnp.zeros_like(rhs_ref)
    fape_own_ref[...] = jnp.zeros_like(fape_own_ref)
    lane_ids = lax.broadcasted_iota(jnp.int32, (8, BLOCK), 1)

    def back_copy(d):
        return pltpu.make_async_remote_copy(
            src_ref=back_send_ref.at[d],
            dst_ref=back_recv_ref.at[d],
            send_sem=back_send_sem.at[d],
            recv_sem=back_recv_sem.at[d],
            device_id={"res": lax.rem(res - d + res_count, res_count)},
            device_id_type=MESH,
        )

    def one_pair(d, j):
        slot = d * slots + j
        near = near_tab[slot]
        right_t = recv_ref[d, j, :, 0:BLOCK].astype(f32).T.astype(bf16)
        rhs_ref[0:BLOCK, 0:BLOCK] = right_t
        rhs_ref[BLOCK : 2 * BLOCK, BLOCK : 2 * BLOCK] = right_t
        left = left_ref[near]
        left = jnp.concatenate([left[0:64], left[64:128]], axis=1)

        def channels(i, acc):
            base = i * CHUNK
            tiles = []
            for q in range(CHUNK):
                w_row = w_bcast_ref[base + q]
                for g in range(4):
                    tiles.append(left[g * 16 : (g + 1) * 16] * w_row)
            act = jnp.dot(
                jnp.concatenate(tiles, axis=0), rhs_ref[...], preferred_element_type=f32
            )
            for q in range(CHUNK):
                floor = floor_ref[pl.ds(base + q, 1), :]
                gate = gate_ref[pl.ds(base + q, 1), :]
                acc = acc + jnp.maximum(act[q * 64 : (q + 1) * 64], floor) * gate
            return acc

        acc = lax.fori_loop(
            0, 2 * chans // CHUNK, channels, jnp.zeros((64, 2 * BLOCK), f32)
        )
        logit_ref[0:64] = acc[:, 0:BLOCK] + offset
        logit_ref[64:128] = acc[:, BLOCK : 2 * BLOCK] + offset
        geo_t_ref[...] = geo_ref[near].T
        valid = valid_tab[slot].astype(f32)
        far = geo_recv_ref[d, j]

        def geometry(i, fape):
            rows = pl.ds(pl.multiple_of(i * 32, 32), 32)
            geo = geo_t_ref[rows, :]
            gaps = [
                far[m : m + 1] - geo[:, 9 + m : 10 + m] for m in range(3)
            ]
            true_gaps = [
                far[3 + m : 4 + m] - geo[:, 21 + m : 22 + m] for m in range(3)
            ]
            dist_sq = jnp.full((32, BLOCK), 0.0001, f32)
            for k in range(3):
                pred = sum(geo[:, 3 * m + k : 3 * m + k + 1] * gaps[m] for m in range(3))
                true = sum(
                    geo[:, 12 + 3 * m + k : 13 + 3 * m + k] * true_gaps[m] for m in range(3)
                )
                dist_sq = dist_sq + (pred - true) ** 2
            clipped = jnp.minimum(jnp.sqrt(dist_sq), 10.0)
            live = geo[:, 24:25] * (far[6:7] * valid)
            live = jnp.where(geo[:, 25:26] != far[7:8], live, 0.0)
            weight = jax.nn.sigmoid(logit_ref[rows, :]) * live
            weight_ref[rows, :] = weight.astype(bf16)
            scored = weight * clipped
            return fape + scored[0:8] + scored[8:16] + scored[16:24] + scored[24:32]

        fape = lax.fori_loop(0, 4, geometry, jnp.zeros((8, BLOCK), f32))
        fape = jnp.sum(jnp.sum(fape, axis=0, keepdims=True), axis=1, keepdims=True)
        fape = fape * (1.0 / (BLOCK * BLOCK))
        fape_own_ref[...] += jnp.where(lane_ids == pos_tab[slot], fape, 0.0)
        weight = weight_ref[...]
        scale = BLOCK ** (-0.5)
        to_second = lax.dot_general(
            weight, value_ref[near], (((0,), (0,)), ((), ())), preferred_element_type=f32
        )
        back_send_ref[d, j] = (to_second * scale).astype(bf16)
        to_first = jnp.dot(
            weight, recv_ref[d, j, :, BLOCK : 2 * BLOCK], preferred_element_type=f32
        )
        first_ref[d, j] = (to_first * scale).astype(bf16)

    def shard_step(d, carry):
        @pl.when(d > 0)
        def _():
            for copy in row_copies(d):
                copy.wait()

        def pair_step(j, inner):
            one_pair(d, j)
            return inner

        lax.fori_loop(0, slots, pair_step, 0)

        @pl.when(d > 0)
        def _():
            back_copy(d).start()

        return carry

    lax.fori_loop(0, res_count, shard_step, 0)

    fape_copy = pltpu.make_async_remote_copy(
        src_ref=fape_own_ref,
        dst_ref=fape_other_ref,
        send_sem=fape_sems.at[0],
        recv_sem=fape_sems.at[1],
        device_id={"ch": 1 - core},
        device_id_type=MESH,
    )
    fape_copy.start()

    row_id = lax.broadcasted_iota(jnp.int32, (blocks * 16, total * 16), 0)
    col_id = lax.broadcasted_iota(jnp.int32, (blocks * 16, total * 16), 1)
    same_row = (row_id % 16) == (col_id % 16)
    row_block = row_id // 16
    col_slot = lax.broadcasted_iota(jnp.int32, (1, total * 16), 1) // 16

    def spread(table):
        chosen = jnp.zeros((1, total * 16), jnp.int32)
        for s in range(total):
            chosen = jnp.where(col_slot == s, table[s], chosen)
        return jnp.where(same_row & (row_block == chosen), 1.0, 0.0).astype(bf16)

    near_hot = spread(near_tab)
    send_hot = spread(send_tab)

    def wait_back(d, carry):
        back_copy(d).wait()
        return carry

    def near_part(g):
        tiles = first_ref[:, :, g * 16 : (g + 1) * 16, :].reshape(total * 16, BLOCK)
        return jnp.dot(near_hot, tiles, preferred_element_type=f32)

    for g in range(BLOCK // 16):
        delta_ref[:, g * 16 : (g + 1) * 16, :] = near_part(g).reshape(blocks, 16, BLOCK)

    lax.fori_loop(1, res_count, wait_back, 0)
    back_recv_ref[0] = back_send_ref[0]
    for g in range(BLOCK // 16):
        tiles = back_recv_ref[:, :, g * 16 : (g + 1) * 16, :].reshape(total * 16, BLOCK)
        part = jnp.dot(send_hot, tiles, preferred_element_type=f32)
        delta_ref[:, g * 16 : (g + 1) * 16, :] += part.reshape(blocks, 16, BLOCK)

    half_send_ref[...] = delta_ref[pl.ds((1 - core) * half, half)].astype(bf16)

    half_copy = pltpu.make_async_remote_copy(
        src_ref=half_send_ref,
        dst_ref=half_recv_ref,
        send_sem=half_sems.at[0],
        recv_sem=half_sems.at[1],
        device_id={"ch": 1 - core},
        device_id_type=MESH,
    )
    half_copy.start()
    half_copy.wait()

    def cross_copy(step, i):
        return pltpu.make_async_remote_copy(
            src_ref=cross_send_ref.at[i],
            dst_ref=cross_recv_ref.at[step, i],
            send_sem=cross_send_sem.at[step, i],
            recv_sem=cross_recv_sem.at[step, i],
            device_id={"blk": lax.rem(blk + step, blk_count)},
            device_id_type=MESH,
        )

    def low_copy(i):
        return pltpu.make_async_remote_copy(
            src_ref=low_own_ref.at[i],
            dst_ref=low_other_ref.at[i],
            send_sem=low_send_sem.at[i],
            recv_sem=low_recv_sem.at[i],
            device_id={"ch": 1 - core},
            device_id_type=MESH,
        )

    def cross_start(i, carry):
        own = delta_ref[pl.ds(core * half + i * piece, piece)]
        own = (own + half_recv_ref[pl.ds(i * piece, piece)].astype(f32)).astype(bf16)
        cross_send_ref[i] = own
        cross_recv_ref[0, i] = own
        for step in range(1, blk_count):
            cross_copy(step, i).start()
        return carry

    lax.fori_loop(0, parts, cross_start, 0)

    def write(low, first_block):
        rows = pl.ds(pl.multiple_of(first_block * BLOCK, BLOCK), piece * BLOCK)
        low = low.reshape(piece * BLOCK, BLOCK)
        grown = jnp.dot(low, w_out_ref[...], preferred_element_type=f32)
        updated_ref[rows, :] = (single_ref[rows, :].astype(f32) + grown).astype(bf16)

    def own_piece(i, carry):
        for step in range(1, blk_count):
            cross_copy(step, i).wait()
        terms = [
            cross_recv_ref[lax.rem(blk - x + blk_count, blk_count), i].astype(f32)
            for x in range(blk_count)
        ]
        low_own_ref[i] = sum(terms[1:], terms[0]).astype(bf16)
        low_copy(i).start()
        write(low_own_ref[i], core * half + i * piece)
        return carry

    lax.fori_loop(0, parts, own_piece, 0)

    fape_copy.wait()
    fape_ref[...] = fape_own_ref[...] + fape_other_ref[...]

    def other_piece(i, carry):
        low_copy(i).wait()
        write(low_other_ref[i], (1 - core) * half + i * piece)
        return carry

    lax.fori_loop(0, parts, other_piece, 0)


def shards(
    single,
    frames,
    teacher,
    res_mask,
    chain_ids,
    block_pairs,
    w_left,
    w_right,
    w_value,
    w_pair,
    pair_bias,
    gate_vec,
    w_out,
):
    res_count = lax.axis_size("res")
    blk_count = lax.axis_size("blk")
    core_count = lax.axis_size("ch")
    row_count, width = single.shape
    blocks = row_count // BLOCK
    pair_dev = block_pairs.shape[1]
    capacity = 1 + (pair_dev + res_count - 2) // res_count
    slots = -(-capacity // core_count)
    chans = w_pair.shape[1]
    parts = 4
    half = blocks // 2
    piece = half // parts
    f32, bf16 = jnp.float32, jnp.bfloat16
    packed = jnp.stack(
        [
            w_pair.T.astype(f32),
            jnp.broadcast_to(-pair_bias[:, None], (chans, BLOCK)),
            jnp.broadcast_to(gate_vec[:, None], (chans, BLOCK)),
        ]
    )
    vmem = pl.BlockSpec(memory_space=pltpu.VMEM)
    smem = pl.BlockSpec(memory_space=pltpu.SMEM)
    dma = pltpu.SemaphoreType.DMA
    total = res_count * slots
    sizes = (res_count, blk_count, blocks, pair_dev, slots, chans, parts)
    updated, fape = pl.pallas_call(
        functools.partial(pair_kernel, sizes),
        out_shape=(
            jax.ShapeDtypeStruct((row_count, width), bf16),
            jax.ShapeDtypeStruct((8, BLOCK), f32),
        ),
        in_specs=[smem] + [vmem] * 10,
        out_specs=(vmem, vmem),
        scratch_shapes=[
            pltpu.VMEM((blocks, BLOCK, BLOCK), bf16),
            pltpu.VMEM((blocks, BLOCK, BLOCK), bf16),
            pltpu.VMEM((blocks, BLOCK, BLOCK), bf16),
            pltpu.VMEM((blocks, 32, BLOCK), f32),
            pltpu.VMEM((blocks, 8, BLOCK), f32),
            pltpu.VMEM((2, 3, chans, BLOCK), f32),
            pltpu.VMEM((2 * chans, 16, 2 * BLOCK), bf16),
            pltpu.VMEM((2 * chans, 2 * BLOCK), f32),
            pltpu.VMEM((2 * chans, 2 * BLOCK), f32),
            pltpu.SMEM((total,), jnp.int32),
            pltpu.SMEM((total,), jnp.int32),
            pltpu.SMEM((total,), jnp.int32),
            pltpu.SMEM((total,), jnp.int32),
            pltpu.VMEM((res_count, slots, BLOCK, 2 * BLOCK), bf16),
            pltpu.VMEM((res_count, slots, BLOCK, 2 * BLOCK), bf16),
            pltpu.VMEM((res_count, slots, 8, BLOCK), f32),
            pltpu.VMEM((res_count, slots, 8, BLOCK), f32),
            pltpu.VMEM((2 * BLOCK, 2 * BLOCK), bf16),
            pltpu.VMEM((BLOCK, BLOCK), f32),
            pltpu.VMEM((BLOCK, 32), f32),
            pltpu.VMEM((BLOCK, BLOCK), bf16),
            pltpu.VMEM((res_count, slots, BLOCK, BLOCK), bf16),
            pltpu.VMEM((res_count, slots, BLOCK, BLOCK), bf16),
            pltpu.VMEM((res_count, slots, BLOCK, BLOCK), bf16),
            pltpu.VMEM((blocks, BLOCK, BLOCK), f32),
            pltpu.VMEM((half, BLOCK, BLOCK), bf16),
            pltpu.VMEM((half, BLOCK, BLOCK), bf16),
            pltpu.VMEM((parts, piece, BLOCK, BLOCK), bf16),
            pltpu.VMEM((blk_count, parts, piece, BLOCK, BLOCK), bf16),
            pltpu.VMEM((parts, piece, BLOCK, BLOCK), bf16),
            pltpu.VMEM((parts, piece, BLOCK, BLOCK), bf16),
            pltpu.VMEM((8, BLOCK), f32),
            pltpu.VMEM((8, BLOCK), f32),
            dma((2,)),
            dma((res_count,)),
            dma((res_count,)),
            dma((res_count,)),
            dma((res_count,)),
            dma((res_count,)),
            dma((res_count,)),
            dma((2,)),
            dma((blk_count, parts)),
            dma((blk_count, parts)),
            dma((parts,)),
            dma((parts,)),
            dma((2,)),
        ],
        compiler_params=pltpu.CompilerParams(
            collective_id=0, has_side_effects=True, vmem_limit_bytes=40 * 1024 * 1024
        ),
    )(
        block_pairs.reshape(-1),
        single,
        frames,
        teacher,
        res_mask[None, :],
        chain_ids[None, :],
        w_left,
        w_right,
        w_value,
        packed,
        w_out,
    )
    return (updated, fape[0, :pair_dev])


def solution(mesh):
    placed = (
        P(("groups", "res"), None),
        P(None, ("groups", "res")),
        P(None, ("groups", "res")),
        P(("groups", "res")),
        P(("groups", "res")),
        P("groups", None, None),
        P(),
        P(),
        P(),
        P(None, "ch"),
        P("ch"),
        P("ch"),
        P(),
    )
    return jax.shard_map(
        shards,
        mesh=mesh,
        in_specs=placed,
        out_specs=(P(("groups", "res"), None), P(("groups", "res", "blk"))),
        check_vma=False,
    )
```

time: 225 us -> 81.1 us (0.36)
  matrix products: 72.7 us -> 0 us
  Pallas kernels: 0 us -> 66.9 us
  waiting for transfers between devices: 39.6 us -> 0 us
  blocking collectives: 27.6 us -> 0 us
  other arithmetic: 23.4 us -> 1.39 us
  local copies, waits for them, and re-layouts: 31 us -> 11.6 us
  starting transfers between devices: 14.7 us -> 0 us
  between operations: 14.7 us -> 0.67 us
    dot_general x32 -> x0, matrix products: 72.7 us -> none  [the longest x12 30.6 us: tile_logit(): jnp.einsum('c,acb->ab', gate_vec, jnp.maximum(pair_act, 0.0), precision=l...]
    pallas_call x0 -> x1, Pallas kernels: none -> 66.9 us  [shards(): pl.pallas_call(functools.partial(pair_kernel, sizes), out_shape=(jax.Shap...]
    all_to_all x3 -> x0, waiting for transfers between devices: 27.9 us -> none  [the longest x1 23.7 us: shards(): lax.all_to_all(row_send, 'res', split_axis=0, concat_axis=0, tiled=True)]
    psum x1 -> x0, blocking collectives: 27.6 us -> none  [shards(): summed_rows = lax.psum(delta_rows, 'blk')]
    all_to_all x3 -> x0, starting transfers between devices: 14.6 us -> none  [the longest x1 6.45 us: shards(): lax.all_to_all(row_send, 'res', split_axis=0, concat_axis=0, tiled=True)]
    psum x1 -> x0, waiting for transfers between devices: 11.7 us -> none  [shards(): logits = lax.psum(partial_logits, 'ch')]
    convert_element_type x16 -> x0, other arithmetic: 10.9 us -> none  [the longest x12 9.25 us: tile_logit(): near_left.astype(jnp.float32)[:, :, None]]
    gather x6 -> x0, local copies, waits for them, and re-layouts: 8.99 us -> none  [the longest x1 2.3 us: shards(): jnp.take(single_blocks, send_local, axis=0)]
  transfers between devices with their start and end apart: 4 -> 0, of which waited for: 3 -> 0; matrix products, arithmetic and copies ran while one was open for 51% -> 0% of each run, Pallas kernels for 0% -> 0%
where the time goes in v1:
time: 81.1 us; the launch traced here: 80.6 us
  Pallas kernels  66.9 us (82%)
  local copies, waits for them, and re-layouts  11.6 us (14%)
  other arithmetic  1.39 us (2%)
    pallas_call x1, Pallas kernels, shards(): pl.pallas_call(functools.partial(pair_kernel, sizes), out_shape=(jax.Shap...  66.9 us
    unnamed x20, local copies, waits for them, and re-layouts  10.1 us

profile of v1, /device:TPU:0, one launch (start us, length us, event | category | flops | bytes accessed | tf_op | source)
XLA Modules:
  0.0 80.6 jit_solution(5860889576168272045)
XLA Ops:
  0.6 0.7 neg.4
  1.3 0.1 stack_broadcast_in_dim.4
  1.4 0.7 convert_bitcast_fusion
  2.1 0.7 stack_broadcast_in_dim.5
  2.8 0.8 %copy.15 = s32[8,12,2]{2,1,0:T(8,128)S(1)} copy(s32[8,12,2]{1,2,0:T(2,128)} %param.18) | data formatting | bytes 1536 | tf_op args[5]
  3.7 0.1 reshape.13.pairs_ref
  3.8 0.0 copy-start
  3.8 1.4 %copy-done = bf16[2048,384]{1,0:T(8,128)(2,1)S(1)} copy-done((bf16[2048,384]{1,0:T(8,128)(2,1)S(1)}, bf16[2048,384]{1,0:T(8,128)(2,1)}, u32[]{:S(2)}) %copy-start) | copy-done | bytes 1572888
  5.2 0.0 copy-start.1
  5.2 0.9 %copy-done.1 = f32[12,2048]{1,0:T(8,128)S(1)} copy-done((f32[12,2048]{1,0:T(8,128)S(1)}, f32[12,2048]{1,0:T(8,128)}, u32[]{:S(2)}) %copy-start.1) | copy-done | bytes 98328
  6.1 0.0 copy-start.2
  6.1 0.9 %copy-done.2 = f32[12,2048]{1,0:T(8,128)S(1)} copy-done((f32[12,2048]{1,0:T(8,128)S(1)}, f32[12,2048]{1,0:T(8,128)}, u32[]{:S(2)}) %copy-start.2) | copy-done | bytes 98328
  7.0 0.0 copy-start.3
  7.0 0.9 %copy-done.3 = bf16[384,128]{1,0:T(8,128)(2,1)S(1)} copy-done((bf16[384,128]{1,0:T(8,128)(2,1)S(1)}, bf16[384,128]{1,0:T(8,128)(2,1)}, u32[]{:S(2)}) %copy-start.3) | copy-done | bytes 98328
  7.9 0.0 copy-start.4
  7.9 0.9 %copy-done.4 = bf16[384,128]{1,0:T(8,128)(2,1)S(1)} copy-done((bf16[384,128]{1,0:T(8,128)(2,1)S(1)}, bf16[384,128]{1,0:T(8,128)(2,1)}, u32[]{:S(2)}) %copy-start.4) | copy-done | bytes 98328
  8.8 0.0 copy-start.5
  8.8 0.9 %copy-done.5 = bf16[384,128]{1,0:T(8,128)(2,1)S(1)} copy-done((bf16[384,128]{1,0:T(8,128)(2,1)S(1)}, bf16[384,128]{1,0:T(8,128)(2,1)}, u32[]{:S(2)}) %copy-start.5) | copy-done | bytes 98328
  9.7 0.0 copy-start.6
  9.7 0.9 %copy-done.6 = bf16[128,384]{1,0:T(8,128)(2,1)S(1)} copy-done((bf16[128,384]{1,0:T(8,128)(2,1)S(1)}, bf16[128,384]{1,0:T(8,128)(2,1)}, u32[]{:S(2)}) %copy-start.6) | copy-done | bytes 98328
  10.6 0.0 copy-start.7
  10.6 0.7 copy-done.7
  11.3 0.0 copy-start.8
  11.3 0.7 copy-done.8
  12.0 66.9 %shard_map.140 = (bf16[2048,384]{1,0:T(8,128)(2,1)S(1)}, f32[8,128]{1,0:T(8,128)S(1)}) custom-call(s32[192]{0:T(256)S(1)} %reshape.13.pairs_ref, bf16[2048,384]{1,0:T(8,128)(2,1)S(1)} %copy-done, f32[12,2048]{1,0:T(8,128)S(1)} %copy-done.1, f32[12,2048]{1,0:T(8,128)S(1)} %copy-done.2, s32[1,2048]{1,0:T(1,128)S(1)} %bitcast.8, s32[1,2048]{1,0:T(1,128)S(1)} %bitcast.9, ...), custom_call_target="tpu_custom_call" | custom-call | tf_op jit(solution)/shard_map/pallas_call | solution.py:485
  78.9 0.5 slice_bitcast_fusion
  79.4 1.1 %copy.17 = bf16[2048,384]{1,0:T(8,128)(2,1)} copy(bf16[2048,384]{1,0:T(8,128)(2,1)S(1)} %get-tuple-element.8) | data formatting | bytes 3145728
  (1 shorter events, 0.0 us)
Async XLA Ops:
  3.8 1.4 %copy-start = (bf16[2048,384]{1,0:T(8,128)(2,1)S(1)}, bf16[2048,384]{1,0:T(8,128)(2,1)}, u32[]{:S(2)}) copy-start(bf16[2048,384]{1,0:T(8,128)(2,1)} %single_ref.1) | copy-start | bytes 4718596
  5.2 0.9 %copy-start.1 = (f32[12,2048]{1,0:T(8,128)S(1)}, f32[12,2048]{1,0:T(8,128)}, u32[]{:S(2)}) copy-start(f32[12,2048]{1,0:T(8,128)} %frames_ref.1) | copy-start | bytes 294916
  6.1 0.9 %copy-start.2 = (f32[12,2048]{1,0:T(8,128)S(1)}, f32[12,2048]{1,0:T(8,128)}, u32[]{:S(2)}) copy-start(f32[12,2048]{1,0:T(8,128)} %teacher_ref.1) | copy-start | bytes 294916
  7.0 0.9 %copy-start.3 = (bf16[384,128]{1,0:T(8,128)(2,1)S(1)}, bf16[384,128]{1,0:T(8,128)(2,1)}, u32[]{:S(2)}) copy-start(bf16[384,128]{1,0:T(8,128)(2,1)} %w_left_ref.1) | copy-start | bytes 294916
  7.9 0.9 %copy-start.4 = (bf16[384,128]{1,0:T(8,128)(2,1)S(1)}, bf16[384,128]{1,0:T(8,128)(2,1)}, u32[]{:S(2)}) copy-start(bf16[384,128]{1,0:T(8,128)(2,1)} %w_right_ref.1) | copy-start | bytes 294916
  8.8 0.9 %copy-start.5 = (bf16[384,128]{1,0:T(8,128)(2,1)S(1)}, bf16[384,128]{1,0:T(8,128)(2,1)}, u32[]{:S(2)}) copy-start(bf16[384,128]{1,0:T(8,128)(2,1)} %w_value_ref.1) | copy-start | bytes 294916
  9.7 0.9 %copy-start.6 = (bf16[128,384]{1,0:T(8,128)(2,1)S(1)}, bf16[128,384]{1,0:T(8,128)(2,1)}, u32[]{:S(2)}) copy-start(bf16[128,384]{1,0:T(8,128)(2,1)} %w_out_ref.1) | copy-start | bytes 294916
  10.6 0.7 copy-start.7
  11.3 0.7 copy-start.8

commit v2 on v1

--- a/solution.py
+++ b/solution.py
@@ -257,7 +257,7 @@
             return acc
 
         acc = lax.fori_loop(
-            0, 2 * chans // CHUNK, channels, jnp.zeros((64, 2 * BLOCK), f32)
+            0, 2 * chans // CHUNK, channels, jnp.zeros((64, 2 * BLOCK), f32), unroll=4
         )
         logit_ref[0:64] = acc[:, 0:BLOCK] + offset
         logit_ref[64:128] = acc[:, BLOCK : 2 * BLOCK] + offset

time: 81.1 us -> 64.6 us (0.80)
  Pallas kernels: 66.9 us -> 50.4 us
    pallas_call x1, Pallas kernels: 66.9 us -> 50.4 us  [shards(): pl.pallas_call(functools.partial(pair_kernel, sizes), out_shape=(jax.Shap...]
where the time goes in v2:
time: 64.6 us; the launch traced here: 64.1 us
  Pallas kernels  50.4 us (78%)
  local copies, waits for them, and re-layouts  11.6 us (18%)
  other arithmetic  1.39 us (2%)
  between operations  0.67 us (1%)
    pallas_call x1, Pallas kernels, shards(): pl.pallas_call(functools.partial(pair_kernel, sizes), out_shape=(jax.Shap...  50.4 us
    unnamed x20, local copies, waits for them, and re-layouts  10.1 us

profile of v2, /device:TPU:0, one launch (start us, length us, event | category | flops | bytes accessed | tf_op | source)
XLA Modules:
  0.0 64.1 jit_solution(12073256059484149346)
XLA Ops:
  0.6 0.7 %neg.4 = f32[64]{0:T(128)S(1)} negate(f32[64]{0:T(128)} %param.23) | non-fusion elementwise | flops 64 | bytes 512 | tf_op jit(solution)/shard_map/neg | solution.py:476
  1.3 0.1 stack_broadcast_in_dim.4
  1.4 0.7 %convert_bitcast_fusion = f32[1,64,128]{2,1,0:T(8,128)S(1)} fusion(bf16[128,64]{0,1:T(8,128)(2,1)} %param.22), kind=kLoop, calls=%fused_computation.1 | loop fusion | flops 8192 | bytes 49152 | tf_op jit(solution)/shard_map/stack | solution.py:473
  2.1 0.7 %stack_broadcast_in_dim.5 = f32[1,64,128]{2,1,0:T(8,128)S(1)} broadcast(f32[64]{0:T(128)} %param.24), dimensions={1} | broadcast | bytes 33024 | tf_op jit(solution)/shard_map/stack;broadcast_in_dim | solution.py:473
  2.8 0.8 %copy.15 = s32[8,12,2]{2,1,0:T(8,128)S(1)} copy(s32[8,12,2]{1,2,0:T(2,128)} %param.18) | data formatting | bytes 1536 | tf_op args[5]
  3.7 0.1 reshape.13.pairs_ref
  3.8 0.0 copy-start
  3.8 1.4 %copy-done = bf16[2048,384]{1,0:T(8,128)(2,1)S(1)} copy-done((bf16[2048,384]{1,0:T(8,128)(2,1)S(1)}, bf16[2048,384]{1,0:T(8,128)(2,1)}, u32[]{:S(2)}) %copy-start) | copy-done | bytes 1572888
  5.2 0.0 copy-start.1
  5.2 0.9 %copy-done.1 = f32[12,2048]{1,0:T(8,128)S(1)} copy-done((f32[12,2048]{1,0:T(8,128)S(1)}, f32[12,2048]{1,0:T(8,128)}, u32[]{:S(2)}) %copy-start.1) | copy-done | bytes 98328
  6.1 0.0 copy-start.2
  6.1 0.9 %copy-done.2 = f32[12,2048]{1,0:T(8,128)S(1)} copy-done((f32[12,2048]{1,0:T(8,128)S(1)}, f32[12,2048]{1,0:T(8,128)}, u32[]{:S(2)}) %copy-start.2) | copy-done | bytes 98328
  7.0 0.0 copy-start.3
  7.0 0.9 %copy-done.3 = bf16[384,128]{1,0:T(8,128)(2,1)S(1)} copy-done((bf16[384,128]{1,0:T(8,128)(2,1)S(1)}, bf16[384,128]{1,0:T(8,128)(2,1)}, u32[]{:S(2)}) %copy-start.3) | copy-done | bytes 98328
  7.9 0.0 copy-start.4
  7.9 0.9 %copy-done.4 = bf16[384,128]{1,0:T(8,128)(2,1)S(1)} copy-done((bf16[384,128]{1,0:T(8,128)(2,1)S(1)}, bf16[384,128]{1,0:T(8,128)(2,1)}, u32[]{:S(2)}) %copy-start.4) | copy-done | bytes 98328
  8.8 0.0 copy-start.5
  8.8 0.9 %copy-done.5 = bf16[384,128]{1,0:T(8,128)(2,1)S(1)} copy-done((bf16[384,128]{1,0:T(8,128)(2,1)S(1)}, bf16[384,128]{1,0:T(8,128)(2,1)}, u32[]{:S(2)}) %copy-start.5) | copy-done | bytes 98328
  9.7 0.0 copy-start.6
  9.7 0.9 %copy-done.6 = bf16[128,384]{1,0:T(8,128)(2,1)S(1)} copy-done((bf16[128,384]{1,0:T(8,128)(2,1)S(1)}, bf16[128,384]{1,0:T(8,128)(2,1)}, u32[]{:S(2)}) %copy-start.6) | copy-done | bytes 98328
  10.6 0.0 copy-start.7
  10.6 0.7 %copy-done.7 = s32[2048]{0:T(1024)S(1)} copy-done((s32[2048]{0:T(1024)S(1)}, s32[2048]{0:T(1024)}, u32[]{:S(2)}) %copy-start.7) | copy-done | bytes 8216
  11.3 0.0 copy-start.8
  11.3 0.7 %copy-done.8 = s32[2048]{0:T(1024)S(1)} copy-done((s32[2048]{0:T(1024)S(1)}, s32[2048]{0:T(1024)}, u32[]{:S(2)}) %copy-start.8) | copy-done | bytes 8216
  12.0 50.4 %shard_map.140 = (bf16[2048,384]{1,0:T(8,128)(2,1)S(1)}, f32[8,128]{1,0:T(8,128)S(1)}) custom-call(s32[192]{0:T(256)S(1)} %reshape.13.pairs_ref, bf16[2048,384]{1,0:T(8,128)(2,1)S(1)} %copy-done, f32[12,2048]{1,0:T(8,128)S(1)} %copy-done.1, f32[12,2048]{1,0:T(8,128)S(1)} %copy-done.2, s32[1,2048]{1,0:T(1,128)S(1)} %bitcast.8, s32[1,2048]{1,0:T(1,128)S(1)} %bitcast.9, ...), custom_call_target="tpu_custom_call" | custom-call | tf_op jit(solution)/shard_map/pallas_call | solution.py:485
  62.4 0.5 slice_bitcast_fusion
  63.0 1.1 %copy.17 = bf16[2048,384]{1,0:T(8,128)(2,1)} copy(bf16[2048,384]{1,0:T(8,128)(2,1)S(1)} %get-tuple-element.8) | data formatting | bytes 3145728
  (1 shorter events, 0.0 us)
Async XLA Ops:
  3.8 1.4 %copy-start = (bf16[2048,384]{1,0:T(8,128)(2,1)S(1)}, bf16[2048,384]{1,0:T(8,128)(2,1)}, u32[]{:S(2)}) copy-start(bf16[2048,384]{1,0:T(8,128)(2,1)} %single_ref.1) | copy-start | bytes 4718596
  5.2 0.9 %copy-start.1 = (f32[12,2048]{1,0:T(8,128)S(1)}, f32[12,2048]{1,0:T(8,128)}, u32[]{:S(2)}) copy-start(f32[12,2048]{1,0:T(8,128)} %frames_ref.1) | copy-start | bytes 294916
  6.1 0.9 %copy-start.2 = (f32[12,2048]{1,0:T(8,128)S(1)}, f32[12,2048]{1,0:T(8,128)}, u32[]{:S(2)}) copy-start(f32[12,2048]{1,0:T(8,128)} %teacher_ref.1) | copy-start | bytes 294916
  7.0 0.9 %copy-start.3 = (bf16[384,128]{1,0:T(8,128)(2,1)S(1)}, bf16[384,128]{1,0:T(8,128)(2,1)}, u32[]{:S(2)}) copy-start(bf16[384,128]{1,0:T(8,128)(2,1)} %w_left_ref.1) | copy-start | bytes 294916
  7.9 0.9 %copy-start.4 = (bf16[384,128]{1,0:T(8,128)(2,1)S(1)}, bf16[384,128]{1,0:T(8,128)(2,1)}, u32[]{:S(2)}) copy-start(bf16[384,128]{1,0:T(8,128)(2,1)} %w_right_ref.1) | copy-start | bytes 294916
  8.8 0.9 %copy-start.5 = (bf16[384,128]{1,0:T(8,128)(2,1)S(1)}, bf16[384,128]{1,0:T(8,128)(2,1)}, u32[]{:S(2)}) copy-start(bf16[384,128]{1,0:T(8,128)(2,1)} %w_value_ref.1) | copy-start | bytes 294916
  9.7 0.9 %copy-start.6 = (bf16[128,384]{1,0:T(8,128)(2,1)S(1)}, bf16[128,384]{1,0:T(8,128)(2,1)}, u32[]{:S(2)}) copy-start(bf16[128,384]{1,0:T(8,128)(2,1)} %w_out_ref.1) | copy-start | bytes 294916
  10.6 0.7 %copy-start.7 = (s32[2048]{0:T(1024)S(1)}, s32[2048]{0:T(1024)}, u32[]{:S(2)}) copy-start(s32[2048]{0:T(1024)} %param.16) | copy-start | bytes 24580
  11.3 0.7 %copy-start.8 = (s32[2048]{0:T(1024)S(1)}, s32[2048]{0:T(1024)}, u32[]{:S(2)}) copy-start(s32[2048]{0:T(1024)} %param.17) | copy-start | bytes 24580

commit v3 on v2

--- a/solution.py
+++ b/solution.py
@@ -154,7 +154,7 @@
         far_geo_ref[n] = jnp.concatenate([frames[9:12], teacher[9:12], mask, chain], axis=0)
         return carry
 
-    lax.fori_loop(0, blocks, features, 0)
+    lax.fori_loop(0, blocks, features, 0, unroll=4)
 
     pl.semaphore_wait(barrier, res_count + blk_count - 1)
 
@@ -257,7 +257,7 @@
             return acc
 
         acc = lax.fori_loop(
-            0, 2 * chans // CHUNK, channels, jnp.zeros((64, 2 * BLOCK), f32), unroll=4
+            0, 2 * chans // CHUNK, channels, jnp.zeros((64, 2 * BLOCK), f32), unroll=2 * chans // CHUNK
         )
         logit_ref[0:64] = acc[:, 0:BLOCK] + offset
         logit_ref[64:128] = acc[:, BLOCK : 2 * BLOCK] + offset
@@ -289,7 +289,7 @@
             scored = weight * clipped
             return fape + scored[0:8] + scored[8:16] + scored[16:24] + scored[24:32]
 
-        fape = lax.fori_loop(0, 4, geometry, jnp.zeros((8, BLOCK), f32))
+        fape = lax.fori_loop(0, 4, geometry, jnp.zeros((8, BLOCK), f32), unroll=2)
         fape = jnp.sum(jnp.sum(fape, axis=0, keepdims=True), axis=1, keepdims=True)
         fape = fape * (1.0 / (BLOCK * BLOCK))
         fape_own_ref[...] += jnp.where(lane_ids == pos_tab[slot], fape, 0.0)

time: 64.6 us -> 59.1 us (0.915)
  Pallas kernels: 50.4 us -> 45 us
    pallas_call x1, Pallas kernels: 50.4 us -> 45 us  [shards(): pl.pallas_call(functools.partial(pair_kernel, sizes), out_shape=(jax.Shap...]
where the time goes in v3:
time: 59.1 us; the launch traced here: 58.6 us
  Pallas kernels  45 us (76%)
  local copies, waits for them, and re-layouts  11.6 us (20%)
  other arithmetic  1.39 us (2%)
  between operations  0.67 us (1%)
    pallas_call x1, Pallas kernels, shards(): pl.pallas_call(functools.partial(pair_kernel, sizes), out_shape=(jax.Shap...  45 us
    unnamed x20, local copies, waits for them, and re-layouts  10.1 us

profile of v3, /device:TPU:0, one launch (start us, length us, event | category | flops | bytes accessed | tf_op | source)
XLA Modules:
  0.0 58.6 jit_solution(7049653951866276728)
XLA Ops:
  0.6 0.7 %neg.4 = f32[64]{0:T(128)S(1)} negate(f32[64]{0:T(128)} %param.23) | non-fusion elementwise | flops 64 | bytes 512 | tf_op jit(solution)/shard_map/neg | solution.py:476
  1.3 0.1 stack_broadcast_in_dim.4
  1.4 0.7 %convert_bitcast_fusion = f32[1,64,128]{2,1,0:T(8,128)S(1)} fusion(bf16[128,64]{0,1:T(8,128)(2,1)} %param.22), kind=kLoop, calls=%fused_computation.1 | loop fusion | flops 8192 | bytes 49152 | tf_op jit(solution)/shard_map/stack | solution.py:473
  2.1 0.7 %stack_broadcast_in_dim.5 = f32[1,64,128]{2,1,0:T(8,128)S(1)} broadcast(f32[64]{0:T(128)} %param.24), dimensions={1} | broadcast | bytes 33024 | tf_op jit(solution)/shard_map/stack;broadcast_in_dim | solution.py:473
  2.8 0.8 %copy.15 = s32[8,12,2]{2,1,0:T(8,128)S(1)} copy(s32[8,12,2]{1,2,0:T(2,128)} %param.18) | data formatting | bytes 1536 | tf_op args[5]
  3.7 0.1 reshape.13.pairs_ref
  3.8 0.0 copy-start
  3.8 1.4 %copy-done = bf16[2048,384]{1,0:T(8,128)(2,1)S(1)} copy-done((bf16[2048,384]{1,0:T(8,128)(2,1)S(1)}, bf16[2048,384]{1,0:T(8,128)(2,1)}, u32[]{:S(2)}) %copy-start) | copy-done | bytes 1572888
  5.2 0.0 copy-start.1
  5.2 0.9 %copy-done.1 = f32[12,2048]{1,0:T(8,128)S(1)} copy-done((f32[12,2048]{1,0:T(8,128)S(1)}, f32[12,2048]{1,0:T(8,128)}, u32[]{:S(2)}) %copy-start.1) | copy-done | bytes 98328
  6.1 0.0 copy-start.2
  6.1 0.9 %copy-done.2 = f32[12,2048]{1,0:T(8,128)S(1)} copy-done((f32[12,2048]{1,0:T(8,128)S(1)}, f32[12,2048]{1,0:T(8,128)}, u32[]{:S(2)}) %copy-start.2) | copy-done | bytes 98328
  7.0 0.0 copy-start.3
  7.0 0.9 %copy-done.3 = bf16[384,128]{1,0:T(8,128)(2,1)S(1)} copy-done((bf16[384,128]{1,0:T(8,128)(2,1)S(1)}, bf16[384,128]{1,0:T(8,128)(2,1)}, u32[]{:S(2)}) %copy-start.3) | copy-done | bytes 98328
  7.9 0.0 copy-start.4
  7.9 0.9 %copy-done.4 = bf16[384,128]{1,0:T(8,128)(2,1)S(1)} copy-done((bf16[384,128]{1,0:T(8,128)(2,1)S(1)}, bf16[384,128]{1,0:T(8,128)(2,1)}, u32[]{:S(2)}) %copy-start.4) | copy-done | bytes 98328
  8.8 0.0 copy-start.5
  8.8 0.9 %copy-done.5 = bf16[384,128]{1,0:T(8,128)(2,1)S(1)} copy-done((bf16[384,128]{1,0:T(8,128)(2,1)S(1)}, bf16[384,128]{1,0:T(8,128)(2,1)}, u32[]{:S(2)}) %copy-start.5) | copy-done | bytes 98328
  9.7 0.0 copy-start.6
  9.7 0.9 %copy-done.6 = bf16[128,384]{1,0:T(8,128)(2,1)S(1)} copy-done((bf16[128,384]{1,0:T(8,128)(2,1)S(1)}, bf16[128,384]{1,0:T(8,128)(2,1)}, u32[]{:S(2)}) %copy-start.6) | copy-done | bytes 98328
  10.6 0.0 copy-start.7
  10.6 0.7 %copy-done.7 = s32[2048]{0:T(1024)S(1)} copy-done((s32[2048]{0:T(1024)S(1)}, s32[2048]{0:T(1024)}, u32[]{:S(2)}) %copy-start.7) | copy-done | bytes 8216
  11.3 0.0 copy-start.8
  11.3 0.7 %copy-done.8 = s32[2048]{0:T(1024)S(1)} copy-done((s32[2048]{0:T(1024)S(1)}, s32[2048]{0:T(1024)}, u32[]{:S(2)}) %copy-start.8) | copy-done | bytes 8216
  12.0 45.0 %shard_map.140 = (bf16[2048,384]{1,0:T(8,128)(2,1)S(1)}, f32[8,128]{1,0:T(8,128)S(1)}) custom-call(s32[192]{0:T(256)S(1)} %reshape.13.pairs_ref, bf16[2048,384]{1,0:T(8,128)(2,1)S(1)} %copy-done, f32[12,2048]{1,0:T(8,128)S(1)} %copy-done.1, f32[12,2048]{1,0:T(8,128)S(1)} %copy-done.2, s32[1,2048]{1,0:T(1,128)S(1)} %bitcast.8, s32[1,2048]{1,0:T(1,128)S(1)} %bitcast.9, ...), custom_call_target="tpu_custom_call" | custom-call | tf_op jit(solution)/shard_map/pallas_call | solution.py:485
  57.0 0.5 slice_bitcast_fusion
  57.5 1.1 %copy.17 = bf16[2048,384]{1,0:T(8,128)(2,1)} copy(bf16[2048,384]{1,0:T(8,128)(2,1)S(1)} %get-tuple-element.8) | data formatting | bytes 3145728
  (1 shorter events, 0.0 us)
Async XLA Ops:
  3.8 1.4 %copy-start = (bf16[2048,384]{1,0:T(8,128)(2,1)S(1)}, bf16[2048,384]{1,0:T(8,128)(2,1)}, u32[]{:S(2)}) copy-start(bf16[2048,384]{1,0:T(8,128)(2,1)} %single_ref.1) | copy-start | bytes 4718596
  5.2 0.9 %copy-start.1 = (f32[12,2048]{1,0:T(8,128)S(1)}, f32[12,2048]{1,0:T(8,128)}, u32[]{:S(2)}) copy-start(f32[12,2048]{1,0:T(8,128)} %frames_ref.1) | copy-start | bytes 294916
  6.1 0.9 %copy-start.2 = (f32[12,2048]{1,0:T(8,128)S(1)}, f32[12,2048]{1,0:T(8,128)}, u32[]{:S(2)}) copy-start(f32[12,2048]{1,0:T(8,128)} %teacher_ref.1) | copy-start | bytes 294916
  7.0 0.9 %copy-start.3 = (bf16[384,128]{1,0:T(8,128)(2,1)S(1)}, bf16[384,128]{1,0:T(8,128)(2,1)}, u32[]{:S(2)}) copy-start(bf16[384,128]{1,0:T(8,128)(2,1)} %w_left_ref.1) | copy-start | bytes 294916
  7.9 0.9 %copy-start.4 = (bf16[384,128]{1,0:T(8,128)(2,1)S(1)}, bf16[384,128]{1,0:T(8,128)(2,1)}, u32[]{:S(2)}) copy-start(bf16[384,128]{1,0:T(8,128)(2,1)} %w_right_ref.1) | copy-start | bytes 294916
  8.8 0.9 %copy-start.5 = (bf16[384,128]{1,0:T(8,128)(2,1)S(1)}, bf16[384,128]{1,0:T(8,128)(2,1)}, u32[]{:S(2)}) copy-start(bf16[384,128]{1,0:T(8,128)(2,1)} %w_value_ref.1) | copy-start | bytes 294916
  9.7 0.9 %copy-start.6 = (bf16[128,384]{1,0:T(8,128)(2,1)S(1)}, bf16[128,384]{1,0:T(8,128)(2,1)}, u32[]{:S(2)}) copy-start(bf16[128,384]{1,0:T(8,128)(2,1)} %w_out_ref.1) | copy-start | bytes 294916
  10.6 0.7 %copy-start.7 = (s32[2048]{0:T(1024)S(1)}, s32[2048]{0:T(1024)}, u32[]{:S(2)}) copy-start(s32[2048]{0:T(1024)} %param.16) | copy-start | bytes 24580
  11.3 0.7 %copy-start.8 = (s32[2048]{0:T(1024)S(1)}, s32[2048]{0:T(1024)}, u32[]{:S(2)}) copy-start(s32[2048]{0:T(1024)} %param.17) | copy-start | bytes 24580

commit v4 on v3

--- a/solution.py
+++ b/solution.py
@@ -14,65 +14,92 @@
 def pair_kernel(
     sizes,
     pairs_ref,
-    single_ref,
-    frames_ref,
-    teacher_ref,
-    mask_ref,
-    chain_ref,
-    w_left_ref,
-    w_right_ref,
-    w_value_ref,
-    gate_in_ref,
-    w_out_ref,
-    updated_ref,
-    fape_ref,
-    left_ref,
-    value_ref,
-    right_ref,
-    geo_ref,
-    far_geo_ref,
-    pack_ref,
-    w_bcast_ref,
-    floor_ref,
-    gate_ref,
-    send_tab,
-    near_tab,
-    valid_tab,
-    pos_tab,
-    send_ref,
-    recv_ref,
-    geo_send_ref,
-    geo_recv_ref,
-    rhs_ref,
-    logit_ref,
-    geo_t_ref,
-    weight_ref,
-    first_ref,
-    back_send_ref,
-    back_recv_ref,
-    delta_ref,
-    half_send_ref,
-    half_recv_ref,
-    cross_send_ref,
-    cross_recv_ref,
-    low_own_ref,
-    low_other_ref,
-    fape_own_ref,
-    fape_other_ref,
-    w_sems,
-    row_send_sem,
-    row_recv_sem,
-    geo_send_sem,
-    geo_recv_sem,
-    back_send_sem,
-    back_recv_sem,
-    half_sems,
-    cross_send_sem,
-    cross_recv_sem,
-    low_send_sem,
-    low_recv_sem,
-    fape_sems,
+    *refs,
 ):
+    inputs, refs = refs[:12], refs[12:]
+    (
+        updated_ref,
+        fape_ref,
+        left_ref,
+        value_ref,
+        right_ref,
+        geo_ref,
+        far_geo_ref,
+        pack_ref,
+        w_bcast_ref,
+        floor_ref,
+        gate_ref,
+        send_tab,
+        near_tab,
+        valid_tab,
+        pos_tab,
+        send_ref,
+        recv_ref,
+        geo_send_ref,
+        geo_recv_ref,
+        rhs_ref,
+        logit_ref,
+        geo_t_ref,
+        weight_ref,
+        first_ref,
+        back_send_ref,
+        back_recv_ref,
+        delta_ref,
+        half_send_ref,
+        half_recv_ref,
+        cross_send_ref,
+        cross_recv_ref,
+        low_own_ref,
+        low_other_ref,
+        fape_own_ref,
+        fape_other_ref,
+        w_sems,
+        row_send_sem,
+        row_recv_sem,
+        geo_send_sem,
+        geo_recv_sem,
+        back_send_sem,
+        back_recv_sem,
+        half_sems,
+        cross_send_sem,
+        cross_recv_sem,
+        low_send_sem,
+        low_recv_sem,
+        fape_sems,
+        single_ref,
+        frames_ref,
+        teacher_ref,
+        mask_ref,
+        chain_ref,
+        w_left_ref,
+        w_right_ref,
+        w_value_ref,
+        w_pair_ref,
+        bias_ref,
+        gate_vec_ref,
+        w_out_ref,
+        load_sems,
+    ) = refs
+    held = (
+        single_ref,
+        frames_ref,
+        teacher_ref,
+        mask_ref,
+        chain_ref,
+        w_left_ref,
+        w_right_ref,
+        w_value_ref,
+        w_pair_ref,
+        bias_ref,
+        gate_vec_ref,
+        w_out_ref,
+    )
+
+    def load(i):
+        return pltpu.make_async_copy(inputs[i], held[i], load_sems.at[i])
+
+    for i in (1, 2, 3, 4, 0, 5, 6, 7, 8, 9, 10, 11):
+        load(i).start()
     res_count, blk_count, blocks, pair_dev, slots, chans, parts = sizes
     total = res_count * slots
     half = blocks // 2
@@ -102,8 +129,6 @@
             device_id={"blk": lax.rem(blk + step, blk_count)},
             device_id_type=MESH,
         )
-
-    pack_ref[0] = gate_in_ref[...]
 
     def lookup(owner, shard):
         base = owner * (pair_dev * 2)
@@ -137,6 +162,11 @@
         return carry
 
     lax.fori_loop(0, res_count, fill_tables, 0)
+    for i in range(12):
+        load(i).wait()
+    pack_ref[0, 0] = w_pair_ref[...].astype(f32)
+    pack_ref[0, 1] = jnp.broadcast_to(-bias_ref[...], (BLOCK, chans)).T
+    pack_ref[0, 2] = jnp.broadcast_to(gate_vec_ref[...], (BLOCK, chans)).T
 
     def features(n, carry):
         rows = single_ref[pl.ds(pl.multiple_of(n * BLOCK, BLOCK), BLOCK), :]
@@ -470,25 +500,33 @@
     half = blocks // 2
     piece = half // parts
     f32, bf16 = jnp.float32, jnp.bfloat16
-    packed = jnp.stack(
-        [
-            w_pair.T.astype(f32),
-            jnp.broadcast_to(-pair_bias[:, None], (chans, BLOCK)),
-            jnp.broadcast_to(gate_vec[:, None], (chans, BLOCK)),
-        ]
-    )
     vmem = pl.BlockSpec(memory_space=pltpu.VMEM)
+    hbm = pl.BlockSpec(memory_space=pltpu.HBM)
     smem = pl.BlockSpec(memory_space=pltpu.SMEM)
     dma = pltpu.SemaphoreType.DMA
     total = res_count * slots
     sizes = (res_count, blk_count, blocks, pair_dev, slots, chans, parts)
+    operands = (
+        single,
+        frames,
+        teacher,
+        res_mask[None, :],
+        chain_ids[None, :],
+        w_left,
+        w_right,
+        w_value,
+        w_pair.T,
+        pair_bias[None, :],
+        gate_vec[None, :],
+        w_out,
+    )
     updated, fape = pl.pallas_call(
         functools.partial(pair_kernel, sizes),
         out_shape=(
             jax.ShapeDtypeStruct((row_count, width), bf16),
             jax.ShapeDtypeStruct((8, BLOCK), f32),
         ),
-        in_specs=[smem] + [vmem] * 10,
+        in_specs=[smem] + [hbm] * len(operands),
         out_specs=(vmem, vmem),
         scratch_shapes=[
             pltpu.VMEM((blocks, BLOCK, BLOCK), bf16),
@@ -537,22 +575,15 @@
             dma((parts,)),
             dma((parts,)),
             dma((2,)),
+            *[pltpu.VMEM(x.shape, x.dtype) for x in operands],
+            dma((len(operands),)),
         ],
         compiler_params=pltpu.CompilerParams(
-            collective_id=0, has_side_effects=True, vmem_limit_bytes=40 * 1024 * 1024
+            collective_id=0, has_side_effects=True, vmem_limit_bytes=63 * 1024 * 1024
         ),
     )(
         block_pairs.reshape(-1),
-        single,
-        frames,
-        teacher,
-        res_mask[None, :],
-        chain_ids[None, :],
-        w_left,
-        w_right,
-        w_value,
-        packed,
-        w_out,
+        *operands,
     )
     return (updated, fape[0, :pair_dev])
 

time: 59.1 us -> 54.4 us (0.920)
  local copies, waits for them, and re-layouts: 11.6 us -> 5.43 us
  Pallas kernels: 45 us -> 48.1 us
  other arithmetic: 1.39 us -> 0 us
    unnamed x20 -> x2, local copies, waits for them, and re-layouts: 10.1 us -> 3.54 us
    pallas_call x1, Pallas kernels: 45 us -> 48.1 us  [shards(): pl.pallas_call(functools.partial(pair_kernel, sizes), out_shape=(jax.Shap...]
    another operation x2 -> x0, local copies, waits for them, and re-layouts: 0.8 us -> none  [shards(): jnp.stack([w_pair.T.astype(f32), jnp.broadcast_to(-pair_bias[:, None], (c...]
    another operation x2 -> x0, other arithmetic: 0.73 us -> none  [shards(): jnp.stack([w_pair.T.astype(f32), jnp.broadcast_to(-pair_bias[:, None], (c...]
    squeeze x1, local copies, waits for them, and re-layouts: 0.51 us -> 1.2 us  [shards(): return (updated, fape[0, :pair_dev])]
    neg x1 -> x0, other arithmetic: 0.66 us -> none  [shards(): -pair_bias[:, None]]
where the time goes in v4:
time: 54.4 us; the launch traced here: 54.2 us
  Pallas kernels  48.1 us (88%)
  local copies, waits for them, and re-layouts  5.43 us (10%)
  between operations  0.64 us (1%)
    pallas_call x1, Pallas kernels, shards(): pl.pallas_call(functools.partial(pair_kernel, sizes), out_shape=(jax.Shap...  48.1 us
    unnamed x2, local copies, waits for them, and re-layouts  3.54 us
    squeeze x1, local copies, waits for them, and re-layouts, shards(): return (updated, fape[0, :pair_dev])  1.2 us

profile of v4, /device:TPU:0, one launch (start us, length us, event | category | flops | bytes accessed | tf_op | source)
XLA Modules:
  0.0 54.2 jit_solution(3627119660049180249)
XLA Ops:
  0.6 0.8 %copy.15 = s32[8,12,2]{2,1,0:T(8,128)S(1)} copy(s32[8,12,2]{1,2,0:T(2,128)} %param.18) | data formatting | bytes 1536 | tf_op args[5]
  1.5 0.7 %reshape.7.pairs_ref = s32[192]{0:T(256)} reshape(s32[8,12,2]{2,1,0:T(8,128)S(1)} %copy.15) | data formatting | bytes 1536 | tf_op jit(solution)/shard_map/reshape | solution.py:585
  2.2 48.1 %shard_map.140 = (bf16[2048,384]{1,0:T(8,128)(2,1)}, f32[8,128]{1,0:T(8,128)}) custom-call(s32[192]{0:T(256)} %reshape.7.pairs_ref, bf16[2048,384]{1,0:T(8,128)(2,1)} %refs_0_.1, f32[12,2048]{1,0:T(8,128)} %refs_1_.1, f32[12,2048]{1,0:T(8,128)} %refs_2_.1, s32[1,2048]{1,0:T(1,128)} %bitcast.8, s32[1,2048]{1,0:T(1,128)} %bitcast.9, bf16[384,128]{1,0:T(8,128)(2,1)} %refs_5_.1, ...), custom_call_target="tpu_custom_call" | custom-call | tf_op jit(solution)/shard_map/pallas_call | solution.py:523
  50.3 1.2 %slice_bitcast_fusion = f32[12]{0:T(128)} fusion(f32[8,128]{1,0:T(8,128)} %get-tuple-element.5), kind=kLoop, calls=%fused_computation | loop fusion | bytes 96 | tf_op jit(solution)/shard_map/squeeze | solution.py:588
  51.5 2.7 %copy.17 = bf16[2048,384]{1,0:T(8,128)(2,1)} copy(bf16[2048,384]{1,0:T(8,128)(2,1)} %get-tuple-element.8) | data formatting | bytes 3145728

commit v5 on v4

--- a/solution.py
+++ b/solution.py
@@ -319,7 +319,7 @@
             scored = weight * clipped
             return fape + scored[0:8] + scored[8:16] + scored[16:24] + scored[24:32]
 
-        fape = lax.fori_loop(0, 4, geometry, jnp.zeros((8, BLOCK), f32), unroll=2)
+        fape = lax.fori_loop(0, 4, geometry, jnp.zeros((8, BLOCK), f32), unroll=4)
         fape = jnp.sum(jnp.sum(fape, axis=0, keepdims=True), axis=1, keepdims=True)
         fape = fape * (1.0 / (BLOCK * BLOCK))
         fape_own_ref[...] += jnp.where(lane_ids == pos_tab[slot], fape, 0.0)
@@ -399,16 +399,18 @@
 
     half_send_ref[...] = delta_ref[pl.ds((1 - core) * half, half)].astype(bf16)
 
-    half_copy = pltpu.make_async_remote_copy(
-        src_ref=half_send_ref,
-        dst_ref=half_recv_ref,
-        send_sem=half_sems.at[0],
-        recv_sem=half_sems.at[1],
-        device_id={"ch": 1 - core},
-        device_id_type=MESH,
-    )
-    half_copy.start()
-    half_copy.wait()
+    def half_copy(i):
+        return pltpu.make_async_remote_copy(
+            src_ref=half_send_ref.at[pl.ds(i * piece, piece)],
+            dst_ref=half_recv_ref.at[pl.ds(i * piece, piece)],
+            send_sem=half_sems.at[0, i],
+            recv_sem=half_sems.at[1, i],
+            device_id={"ch": 1 - core},
+            device_id_type=MESH,
+        )
+
+    for i in range(parts):
+        half_copy(i).start()
 
     def cross_copy(step, i):
         return pltpu.make_async_remote_copy(
@@ -431,6 +433,7 @@
         )
 
     def cross_start(i, carry):
+        half_copy(i).wait()
         own = delta_ref[pl.ds(core * half + i * piece, piece)]
         own = (own + half_recv_ref[pl.ds(i * piece, piece)].astype(f32)).astype(bf16)
         cross_send_ref[i] = own
@@ -569,7 +572,7 @@
             dma((res_count,)),
             dma((res_count,)),
             dma((res_count,)),
-            dma((2,)),
+            dma((2, parts)),
             dma((blk_count, parts)),
             dma((blk_count, parts)),
             dma((parts,)),

time: 54.4 us -> 52.5 us (0.965)
  Pallas kernels: 48.1 us -> 46.1 us
    pallas_call x1, Pallas kernels: 48.1 us -> 46.1 us  [shards(): pl.pallas_call(functools.partial(pair_kernel, sizes), out_shape=(jax.Shap...]
where the time goes in v5:
time: 52.5 us; the launch traced here: 52.2 us
  Pallas kernels  46.1 us (88%)
  local copies, waits for them, and re-layouts  5.43 us (10%)
  between operations  0.64 us (1%)
    pallas_call x1, Pallas kernels, shards(): pl.pallas_call(functools.partial(pair_kernel, sizes), out_shape=(jax.Shap...  46.1 us
    unnamed x2, local copies, waits for them, and re-layouts  3.54 us
    squeeze x1, local copies, waits for them, and re-layouts, shards(): return (updated, fape[0, :pair_dev])  1.2 us

profile of v5, /device:TPU:0, one launch (start us, length us, event | category | flops | bytes accessed | tf_op | source)
XLA Modules:
  0.0 52.2 jit_solution(16209107442406666679)
XLA Ops:
  0.6 0.8 %copy.15 = s32[8,12,2]{2,1,0:T(8,128)S(1)} copy(s32[8,12,2]{1,2,0:T(2,128)} %param.18) | data formatting | bytes 1536 | tf_op args[5]
  1.5 0.7 %reshape.7.pairs_ref = s32[192]{0:T(256)} reshape(s32[8,12,2]{2,1,0:T(8,128)S(1)} %copy.15) | data formatting | bytes 1536 | tf_op jit(solution)/shard_map/reshape | solution.py:588
  2.2 46.1 %shard_map.140 = (bf16[2048,384]{1,0:T(8,128)(2,1)}, f32[8,128]{1,0:T(8,128)}) custom-call(s32[192]{0:T(256)} %reshape.7.pairs_ref, bf16[2048,384]{1,0:T(8,128)(2,1)} %refs_0_.1, f32[12,2048]{1,0:T(8,128)} %refs_1_.1, f32[12,2048]{1,0:T(8,128)} %refs_2_.1, s32[1,2048]{1,0:T(1,128)} %bitcast.8, s32[1,2048]{1,0:T(1,128)} %bitcast.9, bf16[384,128]{1,0:T(8,128)(2,1)} %refs_5_.1, ...), custom_call_target="tpu_custom_call" | custom-call | tf_op jit(solution)/shard_map/pallas_call | solution.py:526
  48.3 1.2 %slice_bitcast_fusion = f32[12]{0:T(128)} fusion(f32[8,128]{1,0:T(8,128)} %get-tuple-element.5), kind=kLoop, calls=%fused_computation | loop fusion | bytes 96 | tf_op jit(solution)/shard_map/squeeze | solution.py:591
  49.5 2.7 %copy.17 = bf16[2048,384]{1,0:T(8,128)(2,1)} copy(bf16[2048,384]{1,0:T(8,128)(2,1)} %get-tuple-element.8) | data formatting | bytes 3145728
